TPU v7x, 32 devices: a whole 2x2x4 slice. The times are simulated.
32 devices in a mesh: groups: 2 (over y), tensor: 4 (over z), dp: 2 (over x), section: 2 (over core).
Axes of the slice: x: 2, y: 2, z: 4, core: 2. Of those that a mesh axis runs over, the one named last changes fastest.
Arguments:
- queries: bfloat16 [8, 256, 16384], P('groups', 'tensor', ('dp', 'section')), parts along dimension 0, may hold values from -128 to 128
- cache: bfloat16 [4, 8, 256, 256, 128], P('groups', ('dp', 'section'), 'tensor'), parts along dimension 0, may hold values from -6 to 6
- fresh_kv: bfloat16 [8, 2, 8, 256, 128], P('groups', None, ('dp', 'section'), 'tensor'), parts along dimension 0, may hold values from -6 to 6
- lengths: int32 [512], P(('groups', 'tensor')), parts along dimension 0, may hold values from 1 to 256, as said below
- w_out: bfloat16 [16384, 16384], P(('dp', 'section'), 'tensor'), may hold values from -0.375 to 0.375
- residual: bfloat16 [8, 256, 16384], P('groups', ('dp', 'section'), 'tensor'), parts along dimension 0, may hold values from -4 to 4
- layers: bfloat16 [4, 4, 256, 16384], P('groups', None, ('dp', 'section'), 'tensor'), parts along dimension 0, may hold values from -6 to 6
- accepted: int32 [8, 256], P('groups', 'dp'), parts along dimension 0, may hold values from 0 to 1, as said below
- down_map: bfloat16 [3, 16384, 256], P(None, ('tensor', 'section')), may hold values from -0.02734375 to 0.02734375
- up_map: bfloat16 [256, 16384], P(None, ('tensor', 'section')), may hold values from -0.0234375 to 0.0234375
Outputs:
- top_hidden: bfloat16 [8, 256, 16384], P('groups', ('dp', 'section'), 'tensor'), parts along dimension 0
- grad_down: bfloat16 [6, 16384, 256], P('groups', ('tensor', 'section')), parts along dimension 0
- grad_up: bfloat16 [512, 16384], P('groups', ('tensor', 'section')), parts along dimension 0
There are 2 independent parts, one for each index of `groups`. A program takes and returns all parts, laid end to end along the dimension named above; an argument that names none is the same for every part. Nothing has to cross between parts.
Inputs may be any that keep to these rules, and one draw needn't show every extreme that they name: `accepted`: in each decode step every aligned block of the step's rows that one dp and section index holds in the tables' layout of residual accepts 1 to 24 rows, and some block of each step accepts exactly 24. `lengths`: some row's cache is full.
All inputs are finite; a program needn't handle non-finite values.
Results may differ from a plain program's by a relative error of at most 0.012.
Values may be sent and summed in bfloat16 or wider, within the bound.
A program may use at most 256 MiB of HBM per device.

v0:
```python
import math

import jax
import jax.numpy as jnp
from jax import lax
from jax.sharding import PartitionSpec as P


def attend_local(query_rows, cache, new_keys, new_values, valid):
    scaling = 1.0 / math.sqrt(query_rows.shape[-1])
    old_scores = (
        jnp.einsum("rkgd,krld->rkgl", query_rows, cache[0], preferred_element_type=jnp.float32)
        * scaling
    )
    old_scores = jnp.where(valid[:, None, None, :], old_scores, -jnp.inf)
    new_scores = (
        jnp.einsum("rkgd,jkrd->rkgj", query_rows, new_keys, preferred_element_type=jnp.float32)
        * scaling
    )
    highest = jnp.maximum(jnp.max(old_scores, axis=-1), jnp.max(new_scores, axis=-1))
    old_weight = jnp.exp(old_scores - highest[..., None])
    new_weight = jnp.exp(new_scores - highest[..., None])
    totals = jnp.sum(old_weight, axis=-1) + jnp.sum(new_weight, axis=-1)
    old_probs = (old_weight / totals[..., None]).astype(jnp.bfloat16)
    new_probs = (new_weight / totals[..., None]).astype(jnp.bfloat16)
    merged = jnp.einsum("rkgl,krld->rkgd", old_probs, cache[1], preferred_element_type=jnp.float32)
    merged = merged + jnp.einsum(
        "rkgj,jkrd->rkgd", new_probs, new_values, preferred_element_type=jnp.float32
    )
    return merged.astype(jnp.bfloat16)


def on_device(
    queries, cache, fresh_kv, lengths, w_out, residual, layers, accepted, down_map, up_map
):
    steps, tok_rows, head_cols = queries.shape
    kv_local = cache.shape[1]
    head_dim = cache.shape[-1]
    group = head_cols // head_dim // kv_local
    valid = jnp.arange(cache.shape[3], dtype=jnp.int32)[None, :] < lengths[:, None]
    summed_rows = []
    for decode_step in range(steps):
        query_rows = queries[decode_step].reshape(tok_rows, kv_local, group, head_dim)
        attended = attend_local(
            query_rows, cache, fresh_kv[: decode_step + 1, 0], fresh_kv[: decode_step + 1, 1], valid
        )
        attended = attended.reshape(tok_rows, head_cols)
        partial_rows = jnp.dot(
            lax.all_gather(attended, "tensor", axis=0, tiled=True),
            w_out,
            preferred_element_type=jnp.float32,
        )
        summed_rows.append(
            lax.psum_scatter(partial_rows, ("dp", "section"), scatter_dimension=0, tiled=True)
        )
    summed = jnp.stack(summed_rows)
    top_hidden = (residual.astype(jnp.float32) + summed).astype(jnp.bfloat16)
    packed = jnp.stack(
        [layers[0, : steps - 1], layers[1, : steps - 1], top_hidden[: steps - 1], top_hidden[1:]],
        axis=2,
    )
    weight = accepted[: steps - 1].astype(jnp.float32).reshape(-1)
    received = lax.all_to_all(packed, "section", split_axis=3, concat_axis=1, tiled=True)
    count_rows = received.shape[0] * received.shape[1]
    col_width = received.shape[3]
    features = received[:, :, :3].reshape(count_rows, 3, col_width)
    target = received[:, :, 3].reshape(count_rows, col_width)
    pre = lax.psum(
        jnp.einsum("ncj,cjk->nk", features, down_map, preferred_element_type=jnp.float32),
        ("tensor", "section"),
    )
    sigma = jax.nn.sigmoid(pre)
    gated = (pre * sigma).astype(jnp.bfloat16)
    pred = jnp.dot(gated, up_map, preferred_element_type=jnp.float32)
    cotangent = (weight[:, None] * (pred - target.astype(jnp.float32)) / (steps - 1)).astype(
        jnp.bfloat16
    )
    local_up = jnp.einsum("nk,nj->kj", gated, cotangent, preferred_element_type=jnp.float32)
    back = lax.psum(
        jnp.einsum("nj,kj->nk", cotangent, up_map, preferred_element_type=jnp.float32),
        ("tensor", "section"),
    )
    dpre = (back * sigma * (1.0 + pre * (1.0 - sigma))).astype(jnp.bfloat16)
    local_down = jnp.einsum("ncj,nk->cjk", features, dpre, preferred_element_type=jnp.float32)
    grad_down, grad_up = (
        lax.psum(local_down.astype(jnp.bfloat16), "dp").astype(jnp.float32),
        lax.psum(local_up.astype(jnp.bfloat16), "dp").astype(jnp.float32),
    )
    return (top_hidden, grad_down.astype(jnp.bfloat16), grad_up.astype(jnp.bfloat16))


def solution(mesh):
    placed = (
        P("groups", "tensor", ("dp", "section")),
        P("groups", ("dp", "section"), "tensor", None, None),
        P("groups", None, ("dp", "section"), "tensor", None),
        P(("groups", "tensor")),
        P(("dp", "section"), "tensor"),
        P("groups", ("dp", "section"), "tensor"),
        P("groups", None, ("dp", "section"), "tensor"),
        P("groups", "dp"),
        P(None, ("tensor", "section"), None),
        P(None, ("tensor", "section")),
    )
    return jax.shard_map(
        on_device,
        mesh=mesh,
        in_specs=placed,
        out_specs=(
            P("groups", ("dp", "section"), "tensor"),
            P("groups", ("tensor", "section"), None),
            P("groups", ("tensor", "section")),
        ),
        check_vma=False,
    )
```

profile of v0, /device:TPU:9, one launch (start us, length us, event | category | flops | bytes accessed | tf_op | source)
XLA Modules:
  0.0 804.4 jit_solution(5103618358941954884)
XLA Ops:
  13.6 9.5 %fusion.69 = (bf16[1,2,64,256,128]{4,3,2,1,0:T(8,128)(2,1)S(1)}, bf16[1,2,64,256,128]{4,3,2,1,0:T(8,128)(2,1)}) fusion(bf16[2,2,64,256,128]{4,3,2,1,0:T(8,128)(2,1)} %param.11), kind=kLoop, calls=%fused_computation.129 | loop fusion | bytes 33554432 | tf_op jit(solution)/shard_map/slice | solution.py:12
  35.8 5.8 fusion.1
  45.4 6.0 fusion.16
  88.7 21.0 %all-gather.11.cloned.1.call-done = bf16[256,4096]{1,0:T(8,128)(2,1)} async-done(((bf16[64,4096]{1,0:T(8,128)(2,1)}), bf16[256,4096]{1,0:T(8,128)(2,1)}) %all-gather.11.cloned.1.call-update) | async-done | bytes 2097168 | tf_op jit(solution)/shard_map/all_gather | solution.py:49
  109.7 17.2 %fusion.79 = f32[256,4096]{1,0:T(8,128)} fusion(bf16[256,4096]{1,0:T(8,128)(2,1)} %all-gather.11.cloned.1.call-done, bf16[4096,4096]{1,0:T(8,128)(2,1)} %param.14), kind=kOutput, calls=%fused_computation.139 | convolution fusion | flops 8589934592 | bytes 39845888 | tf_op jit(solution)/shard_map/dot_general | solution.py:48
  127.2 29.3 %all-gather.9.cloned.1.call-done = bf16[256,4096]{1,0:T(8,128)(2,1)} async-done(((bf16[64,4096]{1,0:T(8,128)(2,1)}), bf16[256,4096]{1,0:T(8,128)(2,1)}) %all-gather.9.cloned.1.call-update) | async-done | bytes 2097168 | tf_op jit(solution)/shard_map/all_gather | solution.py:49
  156.5 17.3 %fusion.78 = f32[256,4096]{1,0:T(8,128)} fusion(bf16[256,4096]{1,0:T(8,128)(2,1)} %all-gather.9.cloned.1.call-done, bf16[4096,4096]{1,0:T(8,128)(2,1)} %param.14), kind=kOutput, calls=%fused_computation.138 | convolution fusion | flops 8589934592 | bytes 39845888 | tf_op jit(solution)/shard_map/dot_general | solution.py:48
  173.9 28.9 %all-gather.7.cloned.1.call-done = bf16[256,4096]{1,0:T(8,128)(2,1)} async-done(((bf16[64,4096]{1,0:T(8,128)(2,1)}), bf16[256,4096]{1,0:T(8,128)(2,1)}) %all-gather.7.cloned.1.call-update) | async-done | bytes 2097168 | tf_op jit(solution)/shard_map/all_gather | solution.py:49
  202.8 17.3 %fusion.77 = f32[256,4096]{1,0:T(8,128)} fusion(bf16[256,4096]{1,0:T(8,128)(2,1)} %all-gather.7.cloned.1.call-done, bf16[4096,4096]{1,0:T(8,128)(2,1)} %param.14), kind=kOutput, calls=%fused_computation.137 | convolution fusion | flops 8589934592 | bytes 39845888 | tf_op jit(solution)/shard_map/dot_general | solution.py:48
  220.2 29.3 %all-gather.5.cloned.1.call-done = bf16[256,4096]{1,0:T(8,128)(2,1)} async-done(((bf16[64,4096]{1,0:T(8,128)(2,1)}), bf16[256,4096]{1,0:T(8,128)(2,1)}) %all-gather.5.cloned.1.call-update) | async-done | bytes 2097168 | tf_op jit(solution)/shard_map/all_gather | solution.py:49
  249.5 18.2 %fusion.76 = f32[256,4096]{1,0:T(8,128)} fusion(bf16[256,4096]{1,0:T(8,128)(2,1)} %all-gather.5.cloned.1.call-done, bf16[4096,4096]{1,0:T(8,128)(2,1)} %param.14), kind=kOutput, calls=%fused_computation.136 | convolution fusion | flops 8589934592 | bytes 39845888 | tf_op jit(solution)/shard_map/dot_general | solution.py:48
  271.9 25.0 %reduce-scatter.11.cloned.1.call-done = f32[64,4096]{1,0:T(8,128)} async-done(((f32[256,4096]{1,0:T(8,128)}), f32[64,4096]{1,0:T(8,128)}) %reduce-scatter.11.cloned.1.call-update) | async-done | bytes 1048592 | tf_op jit(solution)/shard_map/reduce_scatter | solution.py:54
  297.0 47.1 %reduce-scatter.9.cloned.1.call-done = f32[64,4096]{1,0:T(8,128)} async-done(((f32[256,4096]{1,0:T(8,128)}), f32[64,4096]{1,0:T(8,128)}) %reduce-scatter.9.cloned.1.call-update) | async-done | bytes 1048592 | tf_op jit(solution)/shard_map/reduce_scatter | solution.py:54
  344.1 47.1 %reduce-scatter.7.cloned.1.call-done = f32[64,4096]{1,0:T(8,128)} async-done(((f32[256,4096]{1,0:T(8,128)}), f32[64,4096]{1,0:T(8,128)}) %reduce-scatter.7.cloned.1.call-update) | async-done | bytes 1048592 | tf_op jit(solution)/shard_map/reduce_scatter | solution.py:54
  391.2 47.2 %reduce-scatter.5.cloned.1.call-done = f32[64,4096]{1,0:T(8,128)} async-done(((f32[256,4096]{1,0:T(8,128)}), f32[64,4096]{1,0:T(8,128)}) %reduce-scatter.5.cloned.1.call-update) | async-done | bytes 1048592 | tf_op jit(solution)/shard_map/reduce_scatter | solution.py:54
  447.7 18.6 %copy.106 = bf16[3,64,4,4096]{1,2,0,3:T(4,128)(2,1)} copy(bf16[3,64,4,4096]{3,1,0,2:T(8,128)(2,1)} %pad_maximum_fusion) | data formatting | bytes 12582912 | tf_op jit(solution)/shard_map/stack | solution.py:58
  466.3 18.6 %reshape.112 = bf16[2,2,786432]{2,1,0:T(2,128)(2,1)} reshape(bf16[4096,3,4,64]{3,2,1,0:T(4,128)(2,1)} %bitcast.161) | data formatting | bytes 12582912
  484.9 15.8 %all_to_all.18 = bf16[2,2,786432]{2,1,0:T(2,128)(2,1)} all-to-all(bf16[2,2,786432]{2,1,0:T(2,128)(2,1)} %reshape.112), channel_id=1, replica_groups=mesh['groups'=2,'tensor'=4,'dp'=2,'section'=2] {'section'}, dimensions={0} | all-to-all | bytes 12582912 | tf_op jit(solution)/shard_map/all_to_all | solution.py:63
  500.6 18.3 %reshape.113 = bf16[4096,3,4,64]{3,2,1,0:T(4,128)(2,1)} reshape(bf16[2,2,786432]{2,1,0:T(2,128)(2,1)} %all_to_all.18) | data formatting | bytes 12582912
  519.0 31.6 %copy.114 = bf16[3,64,4,2,2048]{4,3,1,2,0:T(2,128)(2,1)} copy(bf16[3,64,4,2,2048]{1,2,0,4,3:T(4,128)(2,1)} %bitcast.162) | data formatting | bytes 12582912 | tf_op jit(solution)/shard_map/all_to_all | solution.py:63
  566.9 50.3 %all-reduce.5.cloned.1.call-done = f32[384,256]{1,0:T(8,128)} async-done(((f32[384,256]{1,0:T(8,128)}), f32[384,256]{1,0:T(8,128)}) %all-reduce.5.cloned.1.call-update) | async-done | bytes 393232 | tf_op jit(solution)/shard_map/psum | solution.py:68
  625.8 51.1 %all-reduce.7.cloned.1.call-done = f32[384,256]{1,0:T(8,128)} async-done(((f32[384,256]{1,0:T(8,128)}), f32[384,256]{1,0:T(8,128)}) %all-reduce.7.cloned.1.call-update) | async-done | bytes 393232 | tf_op jit(solution)/shard_map/psum | solution.py:79
  676.9 6.0 convolution_convert_fusion
  683.0 109.6 %all-reduce.9.cloned.1.call-done = (bf16[3,2048,256]{2,1,0:T(8,128)(2,1)}, bf16[256,2048]{1,0:T(8,128)(2,1)}) async-done(((bf16[3,2048,256]{2,1,0:T(8,128)(2,1)}, bf16[256,2048]{1,0:T(8,128)(2,1)}), (bf16[3,2048,256]{2,1,0:T(8,128)(2,1)}, bf16[256,2048]{1,0:T(8,128)(2,1)})) %all-reduce.9.cloned.1.call-update) | async-done | bytes 4194320 | tf_op jit(solution)/shard_map/psum | solution.py:86
  (158 shorter events, 103.1 us)
Async XLA Ops:
  7.2 554.7 %copy-start = (bf16[3,2048,256]{2,1,0:T(8,128)(2,1)S(1)}, bf16[3,2048,256]{2,1,0:T(8,128)(2,1)}, u32[]{:S(2)}) copy-start(bf16[3,2048,256]{2,1,0:T(8,128)(2,1)} %param.18) | copy-start | bytes 9437188
  7.2 102.5 %all-gather.11.cloned.1.call-start = ((), (), s32[]{:S(2)}) async-start(), calls=%async_computation.11 | async-start | bytes 2621440 | tf_op jit(solution)/shard_map/all_gather | solution.py:49
  13.6 9.5 %copy-start.9 = (bf16[4,64,4096]{2,1,0:T(8,128)(2,1)S(1)}, bf16[4,64,4096]{2,1,0:T(8,128)(2,1)}, u32[]{:S(2)}) copy-start(bf16[4,64,4096]{2,1,0:T(8,128)(2,1)} %param.10) | copy-start | bytes 6291460
  32.2 9.4 %copy-start.21 = (f32[64,2,16]{0,2,1:T(8,128)}, f32[64,2,16]{0,2,1:T(8,128)S(1)}, u32[]{:S(2)}) copy-start(f32[64,2,16]{0,2,1:T(8,128)S(1)} %copy.93) | copy-start | bytes 24580
  33.8 7.9 copy-start.23
  34.5 10.8 %slice-start = ((s8[8388608]{0:T(1024)(128)(4,1)}), s8[4194304]{0:T(1024)(128)(4,1)S(1)}, s32[]{:S(2)}) async-start(s8[8388608]{0:T(1024)(128)(4,1)} %bitcast.159), calls=%async_computation.16 | async-start | bytes 8388608
  35.8 5.9 copy-start.10
  35.8 7.3 copy-start.12
  35.8 7.3 copy-start.27
  35.8 9.5 %slice-start.1 = ((s8[8388608]{0:T(1024)(128)(4,1)}), s8[4194304]{0:T(1024)(128)(4,1)S(1)}, s32[]{:S(2)}) async-start(s8[8388608]{0:T(1024)(128)(4,1)} %bitcast.159), calls=%async_computation.17 | async-start | bytes 8388608
  41.6 12.7 %copy-start.4 = (f32[64,2,16,256]{3,2,1,0:T(8,128)}, f32[64,2,16,256]{3,2,1,0:T(8,128)S(1)}, u32[]{:S(2)}) copy-start(f32[64,2,16,256]{3,2,1,0:T(8,128)S(1)} %fusion.1) | copy-start | bytes 6291460
  44.2 9.8 %copy-start.18 = (f32[64,2,16,4]{2,3,1,0:T(4,128)}, f32[64,2,16,4]{2,3,1,0:T(4,128)S(1)}, u32[]{:S(2)}) copy-start(f32[64,2,16,4]{2,3,1,0:T(4,128)S(1)} %get-tuple-element.40) | copy-start | bytes 98308
  64.3 92.2 %all-gather.9.cloned.1.call-start = ((), (), s32[]{:S(2)}) async-start(), calls=%async_computation.9 | async-start | bytes 2621440 | tf_op jit(solution)/shard_map/all_gather | solution.py:49
  66.2 5.6 copy-start.17
  73.2 129.6 %all-gather.7.cloned.1.call-start = ((), (), s32[]{:S(2)}) async-start(), calls=%async_computation.7 | async-start | bytes 2621440 | tf_op jit(solution)/shard_map/all_gather | solution.py:49
  73.5 5.7 copy-start.30
  80.7 168.8 %all-gather.5.cloned.1.call-start = ((), (), s32[]{:S(2)}) async-start(), calls=%async_computation.5 | async-start | bytes 2621440 | tf_op jit(solution)/shard_map/all_gather | solution.py:49
  88.6 208.4 %reduce-scatter.11.cloned.1.call-start = ((), (), s32[]{:S(2)}) async-start(), calls=%async_computation.12 | async-start | bytes 5242880 | tf_op jit(solution)/shard_map/reduce_scatter | solution.py:54
  127.0 217.1 %reduce-scatter.9.cloned.1.call-start = ((), (), s32[]{:S(2)}) async-start(), calls=%async_computation.10 | async-start | bytes 5242880 | tf_op jit(solution)/shard_map/reduce_scatter | solution.py:54
  173.9 217.3 %reduce-scatter.7.cloned.1.call-start = ((), (), s32[]{:S(2)}) async-start(), calls=%async_computation.8 | async-start | bytes 5242880 | tf_op jit(solution)/shard_map/reduce_scatter | solution.py:54
  220.1 218.3 %reduce-scatter.5.cloned.1.call-start = ((), (), s32[]{:S(2)}) async-start(), calls=%async_computation.6 | async-start | bytes 5242880 | tf_op jit(solution)/shard_map/reduce_scatter | solution.py:54
  267.8 349.4 %all-reduce.5.cloned.1.call-start = ((), (), s32[]{:S(2)}) async-start(), calls=%async_computation.13 | async-start | bytes 786432 | tf_op jit(solution)/shard_map/psum | solution.py:68
  564.1 112.9 %all-reduce.7.cloned.1.call-start = ((), (), s32[]{:S(2)}) async-start(), calls=%async_computation.14 | async-start | bytes 786432 | tf_op jit(solution)/shard_map/psum | solution.py:79
  622.3 170.3 %all-reduce.9.cloned.1.call-start = ((), (), s32[]{:S(2)}) async-start(), calls=%async_computation.15 | async-start | bytes 8388608 | tf_op jit(solution)/shard_map/psum | solution.py:86
  (24 other events, 71.7 us)
Sparse Core Ops, SparseCore 0:
  64.4 45.2 all-gather.10
  111.8 44.6 all-gather.8
  158.1 44.6 all-gather.6
  204.8 44.6 all-gather.4
  251.9 45.0 reduce-scatter.10
  299.5 44.5 reduce-scatter.8
  346.6 44.5 reduce-scatter.6
  393.9 44.5 reduce-scatter.4
  564.2 52.9 all-reduce.4
  622.4 54.4 all-reduce.6
  683.1 109.4 all-reduce.8
where the time goes:
time: 816 us; the launch traced here: 804 us
  waiting for transfers between devices  486 us (60%)
  local copies, waits for them, and re-layouts  137 us (17%)
  matrix products  132 us (16%)
  other arithmetic  16.8 us (2%)
  blocking collectives  15.8 us (2%)
  between operations  15 us (2%)
    reduce_scatter x4, waiting for transfers between devices, on_device(): lax.psum_scatter(partial_rows, ('dp', 'section'), scatter_dimension=0, ti...  166 us
    psum x1, waiting for transfers between devices, on_device(): lax.psum(local_down.astype(jnp.bfloat16), 'dp').astype(jnp.float32)  110 us
    all_gather x4, waiting for transfers between devices, on_device(): lax.all_gather(attended, 'tensor', axis=0, tiled=True)  109 us
    dot_general x4, matrix products, on_device(): jnp.dot(lax.all_gather(attended, 'tensor', axis=0, tiled=True), w_out, pr...  70.1 us
    unnamed x87, local copies, waits for them, and re-layouts  56.7 us
    psum x1, waiting for transfers between devices, on_device(): lax.psum(jnp.einsum('nj,kj->nk', cotangent, up_map, preferred_element_typ...  51.1 us
    psum x1, waiting for transfers between devices, on_device(): lax.psum(jnp.einsum('ncj,cjk->nk', features, down_map, preferred_element_...  50.3 us
    all_to_all x2, local copies, waits for them, and re-layouts, on_device(): lax.all_to_all(packed, 'section', split_axis=3, concat_axis=1, tiled=True)  37.3 us
  transfers between devices with their start and end apart: 11, of which 11 were waited for; matrix products, arithmetic and copies ran while one was open for 13% of the time, Pallas kernels for 0%

commit v1 on v0

v1 whole, which is shorter than its diff:
```python
import functools
import math

import jax
import jax.numpy as jnp
from jax import lax
from jax.experimental import pallas as pl
from jax.experimental.pallas import tpu as pltpu
from jax.sharding import PartitionSpec as P

MOST = 24
MESH = pl.DeviceIdType.MESH
BF16 = jnp.bfloat16
F32 = jnp.float32


def attend_kernel(group, q_ref, cache_ref, fresh_ref, bias_ref, out_ref):
    scaling = 1.0 / math.sqrt(q_ref.shape[-1])
    q = q_ref[:, 0]
    old = jnp.einsum("rqd,rld->rql", q, cache_ref[0, 0], preferred_element_type=F32)
    old = old * scaling + bias_ref[...]
    new = jnp.einsum("rqd,rjd->rqj", q, fresh_ref[0, 0], preferred_element_type=F32)
    step = lax.broadcasted_iota(jnp.int32, new.shape, 1) // group
    seen = lax.broadcasted_iota(jnp.int32, new.shape, 2) <= step
    new = jnp.where(seen, new * scaling, -jnp.inf)
    highest = jnp.maximum(
        jnp.max(old, axis=-1, keepdims=True), jnp.max(new, axis=-1, keepdims=True)
    )
    old = jnp.exp(old - highest)
    new = jnp.exp(new - highest)
    total = jnp.sum(old, axis=-1, keepdims=True) + jnp.sum(new, axis=-1, keepdims=True)
    share = 1.0 / total
    old = (old * share).astype(BF16)
    new = (new * share).astype(BF16)
    merged = jnp.einsum("rql,rld->rqd", old, cache_ref[1, 0], preferred_element_type=F32)
    merged += jnp.einsum("rqj,rjd->rqd", new, fresh_ref[1, 0], preferred_element_type=F32)
    out_ref[:, 0] = merged.astype(BF16)


def attend(queries, cache, fresh_kv, lengths):
    steps, rows, head_cols = queries.shape
    kv, span, dim = cache.shape[1], cache.shape[3], cache.shape[4]
    group = head_cols // dim // kv
    each = 8
    q = queries.reshape(steps, rows, kv, group, dim).transpose(1, 2, 0, 3, 4)
    q = q.reshape(rows, kv, steps * group, dim)
    fresh = fresh_kv.transpose(1, 2, 3, 0, 4)
    fresh = jnp.pad(fresh, ((0, 0), (0, 0), (0, 0), (0, 16 - steps), (0, 0)))
    held = jnp.arange(span, dtype=jnp.int32)[None, None, :] < lengths[:, None, None]
    bias = jnp.where(held, 0.0, -jnp.inf).astype(F32)
    out = pl.pallas_call(
        functools.partial(attend_kernel, group),
        grid=(kv, rows // each),
        in_specs=[
            pl.BlockSpec((each, 1, steps * group, dim), lambda k, i: (i, k, 0, 0)),
            pl.BlockSpec((2, 1, each, span, dim), lambda k, i: (0, k, i, 0, 0)),
            pl.BlockSpec((2, 1, each, 16, dim), lambda k, i: (0, k, i, 0, 0)),
            pl.BlockSpec((each, 1, span), lambda k, i: (i, 0, 0)),
        ],
        out_specs=pl.BlockSpec((each, 1, steps * group, dim), lambda k, i: (i, k, 0, 0)),
        out_shape=jax.ShapeDtypeStruct((rows, kv, steps * group, dim), BF16),
        compiler_params=pltpu.CompilerParams(vmem_limit_bytes=32 * 2**20),
        cost_estimate=pl.CostEstimate(
            flops=4 * rows * kv * steps * group * span * dim,
            bytes_accessed=2 * cache.size + 4 * queries.size,
            transcendentals=rows * kv * steps * group * span,
        ),
    )(q, cache, fresh, bias)
    out = out.reshape(rows, kv, steps, group, dim).transpose(2, 0, 1, 3, 4)
    return out.reshape(steps, rows, head_cols)


def project_kernel(
    n_t, n_dp, n_sec, att_ref, w_ref, res_ref, top_ref,
    held, w_vmem, acc, part, own, got,
    w_sem, local_sem, gs_sem, gr_sem, rs_sem, rr_sem,
):
    steps, rows, depth = att_ref.shape
    cols = w_ref.shape[1]
    blocks = n_dp * n_sec
    owned = res_ref.shape[1]
    halves, half = got.shape[1], got.shape[4]
    tile = 512
    t = lax.axis_index("tensor")
    me = lax.axis_index("dp") * n_sec + lax.axis_index("section")

    w_copies = [
        pltpu.make_async_copy(
            w_ref.at[:, pl.ds(h * half, half)], w_vmem.at[:, pl.ds(h * half, half)], w_sem.at[h]
        )
        for h in range(halves)
    ]
    locals_ = [
        pltpu.make_async_copy(att_ref.at[s], held.at[s, t], local_sem.at[s]) for s in range(steps)
    ]

    def other(k):
        return lax.rem(t + k, n_t)

    def peer(k):
        b = lax.rem(me + k, blocks)
        return b, {"dp": b // n_sec, "section": lax.rem(b, n_sec)}

    barrier = pltpu.get_barrier_semaphore()
    for k in range(1, n_t):
        pl.semaphore_signal(
            barrier, inc=1, device_id={"tensor": other(k)}, device_id_type=MESH
        )
    for k in range(1, blocks):
        pl.semaphore_signal(barrier, inc=1, device_id=peer(k)[1], device_id_type=MESH)
    pl.semaphore_wait(barrier, n_t - 1 + blocks - 1)

    def gather(s, k):
        return pltpu.make_async_remote_copy(
            src_ref=att_ref.at[s],
            dst_ref=held.at[s, t],
            send_sem=gs_sem.at[s, k - 1],
            recv_sem=gr_sem.at[s, k - 1],
            device_id={"tensor": other(k)},
            device_id_type=MESH,
        )

    def scatter(s, h, k):
        return pltpu.make_async_remote_copy(
            src_ref=part.at[s % 2, h, k - 1],
            dst_ref=got.at[s, h, k - 1],
            send_sem=rs_sem.at[s, h, k - 1],
            recv_sem=rr_sem.at[s, h, k - 1],
            device_id=peer(k)[1],
            device_id_type=MESH,
        )

    def start_gather(s):
        for k in range(n_t - 1, 0, -1):
            gather(s, k).start()

    def finish(s):
        for h in range(halves):
            for k in range(1, blocks):
                scatter(s, h, k).wait_recv()
            for c in range(0, half, tile):
                at = pl.ds(h * half + c, tile)
                total = own[s % 2, :, at] + res_ref[s, :, at].astype(F32)
                for k in range(1, blocks):
                    total += got[s, h, k - 1, :, pl.ds(c, tile)].astype(F32)
                top_ref[s, :, at] = total.astype(BF16)

    start_gather(0)
    for c in locals_:
        c.start()
    for c in w_copies:
        c.start()
    if steps > 1:
        start_gather(1)
    for c in locals_:
        c.wait()
    for s in range(steps):
        for k in range(1, n_t):
            gather(s, k).wait_recv()
        if s + 2 < steps:
            start_gather(s + 2)
        if s == 0:
            for c in w_copies:
                c.wait()
        if s >= 2:
            for h in range(halves):
                for k in range(1, blocks):
                    scatter(s - 2, h, k).wait_send()
        for h in range(halves):

            def body(i, _, s=s, h=h):
                at = pl.ds(pl.multiple_of(i * tile, tile), tile)
                wide = pl.ds(pl.multiple_of(h * half + i * tile, tile), tile)
                lhs = held[s].reshape(n_t * rows, depth)
                prod = jnp.dot(lhs, w_vmem[:, wide], preferred_element_type=F32)
                acc[...] = prod
                own[s % 2, :, wide] = acc[pl.ds(pl.multiple_of(me * owned, owned), owned), :]
                for k in range(1, blocks):
                    b = peer(k)[0]
                    part[s % 2, h, k - 1, :, at] = acc[
                        pl.ds(pl.multiple_of(b * owned, owned), owned), :
                    ].astype(BF16)
                return 0

            lax.fori_loop(0, half // tile, body, 0)
            for k in range(1, blocks):
                scatter(s, h, k).start()
        if s >= 1:
            finish(s - 1)
    finish(steps - 1)
    for s in range(max(0, steps - 2), steps):
        for h in range(halves):
            for k in range(1, blocks):
                scatter(s, h, k).wait_send()
    for s in range(steps):
        for k in range(1, n_t):
            gather(s, k).wait_send()


def project(mesh_shape, attended, w_out, residual):
    steps, rows, depth = attended.shape
    cols = w_out.shape[1]
    n_t, n_dp, n_sec = mesh_shape["tensor"], mesh_shape["dp"], mesh_shape["section"]
    blocks = n_dp * n_sec
    owned = residual.shape[1]
    if rows % 16 or owned % 16 or cols % 1024 or n_t < 2 or blocks < 2:
        whole = lax.all_gather(attended, "tensor", axis=1, tiled=True)
        partial_rows = jnp.einsum("srj,jk->srk", whole, w_out, preferred_element_type=F32)
        summed = lax.psum_scatter(
            partial_rows, ("dp", "section"), scatter_dimension=1, tiled=True
        )
        return (residual.astype(F32) + summed).astype(BF16)
    halves = 2
    half = cols // halves
    dma = pltpu.SemaphoreType.DMA
    return pl.pallas_call(
        functools.partial(project_kernel, n_t, n_dp, n_sec),
        out_shape=jax.ShapeDtypeStruct(residual.shape, BF16),
        in_specs=[
            pl.BlockSpec(memory_space=pl.ANY),
            pl.BlockSpec(memory_space=pl.ANY),
            pl.BlockSpec(memory_space=pltpu.VMEM),
        ],
        out_specs=pl.BlockSpec(memory_space=pltpu.VMEM),
        scratch_shapes=[
            pltpu.VMEM((steps, n_t, rows, depth), BF16),
            pltpu.VMEM((depth, cols), BF16),
            pltpu.VMEM((n_t * rows, 512), F32),
            pltpu.VMEM((2, halves, blocks - 1, owned, half), BF16),
            pltpu.VMEM((2, owned, cols), F32),
            pltpu.VMEM((steps, halves, blocks - 1, owned, half), BF16),
            dma((halves,)),
            dma((steps,)),
            dma((steps, n_t - 1)),
            dma((steps, n_t - 1)),
            dma((steps, halves, blocks - 1)),
            dma((steps, halves, blocks - 1)),
        ],
        compiler_params=pltpu.CompilerParams(
            collective_id=0, has_side_effects=True, vmem_limit_bytes=61 * 2**20
        ),
        cost_estimate=pl.CostEstimate(
            flops=2 * steps * rows * n_t * depth * cols,
            bytes_accessed=2 * w_out.size,
            transcendentals=0,
        ),
    )(attended, w_out, residual)


def on_device(
    mesh_shape, queries, cache, fresh_kv, lengths, w_out, residual, layers, accepted, down_map, up_map
):
    steps = queries.shape[0]
    n_t, n_dp, n_sec = mesh_shape["tensor"], mesh_shape["dp"], mesh_shape["section"]
    blocks = n_dp * n_sec
    owned = residual.shape[1]
    section = lax.axis_index("section")
    rank_width = up_map.shape[0]
    col_width = up_map.shape[1]

    most = min(MOST, owned)
    mine = lax.dynamic_slice_in_dim(accepted, section * owned, owned, axis=1)[: steps - 1]
    place = jnp.cumsum(mine, axis=1) - 1
    choose = (place[:, None, :] == jnp.arange(most)[None, :, None]) & (mine[:, None, :] > 0)
    choose = choose.astype(BF16)
    count = (steps - 1) * most

    def compact(x):
        picked = jnp.einsum("smr,srj->smj", choose, x, preferred_element_type=F32)
        return picked.astype(BF16).reshape(count, x.shape[-1])

    def swap(x, k):
        pairs = [(b, (b + k) % blocks) for b in range(blocks)]
        return lax.ppermute(x, ("dp", "section"), pairs)

    def half_for(x, k):
        b = (me + k) % blocks
        return lax.dynamic_slice_in_dim(x, (b % n_sec) * col_width, col_width, axis=x.ndim - 1)

    low_mid = jnp.stack([compact(layers[c, : steps - 1]) for c in range(2)])
    me = lax.axis_index("dp") * n_sec + section

    def in_order(pieces):
        axis = pieces[0].ndim - 2
        size = pieces[0].shape[axis]
        shape = list(pieces[0].shape)
        shape[axis] = blocks * size
        laid = jnp.zeros(shape, pieces[0].dtype)
        for k, piece in enumerate(pieces):
            b = (me + blocks - k) % blocks
            laid = lax.dynamic_update_slice_in_dim(laid, piece, b * size, axis=axis)
        return laid

    low_mid_all = in_order(
        [half_for(low_mid, 0)] + [swap(half_for(low_mid, k), k) for k in range(1, blocks)]
    )
    down_full = lax.all_gather(down_map, "section", axis=1, tiled=True)
    up_full = lax.all_gather(up_map, "section", axis=1, tiled=True)
    gram = lax.psum(
        jnp.einsum("kj,lj->kl", up_map, up_map, preferred_element_type=F32), ("tensor", "section")
    )
    pre_early = jnp.einsum("cnj,cjk->nk", low_mid, down_full[:2], preferred_element_type=F32)

    attended = attend(queries, cache, fresh_kv, lengths)
    top_hidden = project(mesh_shape, attended, w_out, residual)

    top = compact(top_hidden[: steps - 1])
    target = compact(top_hidden[1:])
    pair = jnp.stack([top, target])
    pair_all = in_order([half_for(pair, 0)] + [swap(half_for(pair, k), k) for k in range(1, blocks)])

    pre_part = pre_early + jnp.dot(top, down_full[2], preferred_element_type=F32)
    goal_part = jnp.einsum("nj,kj->nk", target, up_full, preferred_element_type=F32)
    both = jnp.concatenate([pre_part, goal_part], axis=1)
    if n_t <= 4:
        total = both
        for k in range(1, n_t):
            pairs = [(a, (a + k) % n_t) for a in range(n_t)]
            total = total + lax.ppermute(both, "tensor", pairs)
        both = total
    else:
        both = lax.psum(both, "tensor")
    pre, goal = both[:, :rank_width], both[:, rank_width:]
    sigma = jax.nn.sigmoid(pre)
    gated = (pre * sigma).astype(BF16)
    back = jnp.dot(gated.astype(F32), gram, precision=lax.Precision.HIGHEST) - goal
    back = back / (steps - 1)
    dpre = (back * sigma * (1.0 + pre * (1.0 - sigma))).astype(BF16)
    inner = jnp.concatenate([gated, dpre], axis=1)
    inner_all = in_order([inner] + [swap(inner, k) for k in range(1, blocks)])
    gated, dpre = inner_all[:, :rank_width], inner_all[:, rank_width:]

    pred = jnp.dot(gated, up_map, preferred_element_type=F32)
    cotangent = ((pred - pair_all[1].astype(F32)) / (steps - 1)).astype(BF16)
    grad_up = jnp.einsum("nk,nj->kj", gated, cotangent, preferred_element_type=F32).astype(BF16)
    grad_down = jnp.stack(
        [
            jnp.einsum("nj,nk->jk", x, dpre, preferred_element_type=F32).astype(BF16)
            for x in (low_mid_all[0], low_mid_all[1], pair_all[0])
        ]
    )
    return top_hidden, grad_down, grad_up


def solution(mesh):
    placed = (
        P("groups", "tensor", ("dp", "section")),
        P("groups", ("dp", "section"), "tensor", None, None),
        P("groups", None, ("dp", "section"), "tensor", None),
        P(("groups", "tensor")),
        P(("dp", "section"), "tensor"),
        P("groups", ("dp", "section"), "tensor"),
        P("groups", None, ("dp", "section"), "tensor"),
        P("groups", "dp"),
        P(None, ("tensor", "section"), None),
        P(None, ("tensor", "section")),
    )
    return jax.shard_map(
        functools.partial(on_device, dict(mesh.shape)),
        mesh=mesh,
        in_specs=placed,
        out_specs=(
            P("groups", ("dp", "section"), "tensor"),
            P("groups", ("tensor", "section"), None),
            P("groups", ("tensor", "section")),
        ),
        check_vma=False,
    )
```

time: 816 us -> 364 us (0.45); the launches traced: 804 us -> 363 us
  waiting for transfers between devices: 486 us -> 47.3 us
  Pallas kernels: 0 us -> 221 us
  local copies, waits for them, and re-layouts: 137 us -> 27.8 us
  matrix products: 132 us -> 24.8 us
  starting transfers between devices: 1.66 us -> 20.7 us
  blocking collectives: 15.8 us -> 0 us
  other arithmetic: 16.8 us -> 5.61 us
    pallas_call x0 -> x2, Pallas kernels: none -> 221 us  [the longest x1 206 us: project(): pl.pallas_call(functools.partial(project_kernel, n_t, n_dp, n_sec), out_s...]
    psum x3 -> x1, waiting for transfers between devices: 211 us -> 0.03 us  [on_device(): lax.psum(jnp.einsum('kj,lj->kl', up_map, up_map, preferred_element_type=F...]
    reduce_scatter x4 -> x0, waiting for transfers between devices: 166 us -> none  [on_device(): lax.psum_scatter(partial_rows, ('dp', 'section'), scatter_dimension=0, ti...]
    all_gather x4 -> x2, waiting for transfers between devices: 109 us -> 0.02 us  [the longest x1 0.02 us: on_device(): down_full = lax.all_gather(down_map, 'section', axis=1, tiled=True)]
    dot_general x24 -> x13, matrix products: 132 us -> 24.8 us  [the longest x3 8.16 us: on_device(): jnp.einsum('nj,nk->jk', x, dpre, preferred_element_type=F32).astype(BF16)]
    unnamed x87 -> x35, local copies, waits for them, and re-layouts: 56.7 us -> 9.13 us
    ppermute x0 -> x12, waiting for transfers between devices: none -> 45.9 us  [the longest x9 35.2 us: swap(): return lax.ppermute(x, ('dp', 'section'), pairs)]
    all_to_all x2 -> x0, local copies, waits for them, and re-layouts: 37.3 us -> none  [on_device(): lax.all_to_all(packed, 'section', split_axis=3, concat_axis=1, tiled=True)]
  transfers between devices with their start and end apart: 11 -> 15, of which waited for: 11 -> 8; matrix products, arithmetic and copies ran while one was open for 13% -> 10% of each run, Pallas kernels for 0% -> 61%
where the time goes in v1:
time: 364 us; the launch traced here: 363 us
  Pallas kernels  221 us (61%)
  waiting for transfers between devices  47.3 us (13%)
  local copies, waits for them, and re-layouts  27.8 us (8%)
  matrix products  24.8 us (7%)
  starting transfers between devices  20.7 us (6%)
  between operations  16 us (4%)
  other arithmetic  5.61 us (2%)
    pallas_call x1, Pallas kernels, project(): pl.pallas_call(functools.partial(project_kernel, n_t, n_dp, n_sec), out_s...  206 us
    ppermute x9, waiting for transfers between devices, swap(): return lax.ppermute(x, ('dp', 'section'), pairs)  35.2 us
    pallas_call x1, Pallas kernels, attend(): pl.pallas_call(functools.partial(attend_kernel, group), grid=(kv, rows //...  15.2 us
    ppermute x3, starting transfers between devices, on_device(): total = total + lax.ppermute(both, 'tensor', pairs)  14.7 us
    dynamic_update_slice x9, local copies, waits for them, and re-layouts, in_order(): laid = lax.dynamic_update_slice_in_dim(laid, piece, b * size, axis=axis)  11.7 us
    ppermute x3, waiting for transfers between devices, on_device(): total = total + lax.ppermute(both, 'tensor', pairs)  10.7 us
    unnamed x35, local copies, waits for them, and re-layouts  9.13 us
    dot_general x3, matrix products, on_device(): jnp.einsum('nj,nk->jk', x, dpre, preferred_element_type=F32).astype(BF16)  8.16 us
  transfers between devices with their start and end apart: 15, of which 8 were waited for; matrix products, arithmetic and copies ran while one was open for 10% of the time, Pallas kernels for 61%

profile of v1, /device:TPU:9, one launch (start us, length us, event | category | flops | bytes accessed | tf_op | source)
XLA Modules:
  0.0 363.2 jit_solution(7487906533547302529)
XLA Ops:
  12.0 5.8 %copy-done.2 = bf16[2,2,64,256,128]{4,3,2,1,0:T(8,128)(2,1)S(1)} copy-done((bf16[2,2,64,256,128]{4,3,2,1,0:T(8,128)(2,1)S(1)}, bf16[2,2,64,256,128]{4,3,2,1,0:T(8,128)(2,1)}, u32[]{:S(2)}) %copy-start.2) | copy-done | bytes 16777240
  17.8 15.2 %shard_map.121 = bf16[64,2,64,128]{3,2,1,0:T(8,128)(2,1)S(1)} custom-call(bf16[64,2,64,128]{3,2,1,0:T(8,128)(2,1)S(1)} %bitcast.65, bf16[2,2,64,256,128]{4,3,2,1,0:T(8,128)(2,1)S(1)} %copy-done.2, bf16[2,2,64,16,128]{4,3,2,1,0:T(8,128)(2,1)S(1)} %pad.4.fresh_ref, f32[64,1,256]{2,1,0:T(1,128)S(1)} %compare_select_fusion.bias_ref), custom_call_target="tpu_custom_call" | custom-call | flops 1073741824 | bytes 20971520 | tf_op jit(solution)/shard_map/pallas_call | solution.py:51
  33.3 2.3 reshape.73.att_ref
  35.6 205.8 %shard_map.122 = bf16[4,64,4096]{2,1,0:T(8,128)(2,1)} custom-call(bf16[4,64,4096]{2,1,0:T(8,128)(2,1)} %reshape.73.att_ref, bf16[4096,4096]{1,0:T(8,128)(2,1)} %w_ref.1, bf16[4,64,4096]{2,1,0:T(8,128)(2,1)} %res_ref.1), custom_call_target="tpu_custom_call" | custom-call | flops 34359738368 | bytes 33554432 | tf_op jit(solution)/shard_map/pallas_call | solution.py:216
  258.7 7.4 %collective-permute-done = bf16[2,72,2048]{2,1,0:T(8,128)(2,1)} collective-permute-done((bf16[2,72,2048]{2,1,0:T(8,128)(2,1)}, bf16[2,72,2048]{2,1,0:T(8,128)(2,1)}, u32[]{:S(2)}, u32[]{:S(2)}) %collective-permute-start) | collective-permute-done | bytes 589856 | tf_op jit(solution)/shard_map/ppermute | solution.py:274
  266.1 2.0 constant_dynamic-update-slice_fusion.9
  268.0 13.6 %collective-permute-done.10 = bf16[2,72,2048]{2,1,0:T(8,128)(2,1)} collective-permute-done((bf16[2,72,2048]{2,1,0:T(8,128)(2,1)}, bf16[2,72,2048]{2,1,0:T(8,128)(2,1)}, u32[]{:S(2)}, u32[]{:S(2)}) %collective-permute-start.10) | collective-permute-done | bytes 589856 | tf_op jit(solution)/shard_map/ppermute | solution.py:274
  283.6 10.4 %collective-permute-done.1 = bf16[2,72,2048]{2,1,0:T(8,128)(2,1)} collective-permute-done((bf16[2,72,2048]{2,1,0:T(8,128)(2,1)}, bf16[2,72,2048]{2,1,0:T(8,128)(2,1)}, u32[]{:S(2)}, u32[]{:S(2)}) %collective-permute-start.1) | collective-permute-done | bytes 589856 | tf_op jit(solution)/shard_map/ppermute | solution.py:274
  294.0 1.9 constant_dynamic-update-slice_fusion.7
  295.9 2.6 fusion.53
  298.5 3.5 fusion.16
  302.0 2.1 fusion.15
  304.1 11.0 %collective-permute-start.3 = (f32[72,512]{1,0:T(8,128)S(1)}, f32[72,512]{1,0:T(8,128)S(1)}, u32[]{:S(2)}, u32[]{:S(2)}) collective-permute-start(f32[72,512]{1,0:T(8,128)S(1)} %pad_maximum_fusion.5), channel_id=1, source_target_pairs={{0,4},{4,8},{8,12},{12,0},{1,5},{5,9},{9,13},{13,1},{2,6},{6,10},{... | collective-permute-start | bytes 442376 | tf_op jit(solution)/shard_map/ppermute | solution.py:319
  315.1 3.7 %collective-permute-start.4 = (f32[72,512]{1,0:T(8,128)S(1)}, f32[72,512]{1,0:T(8,128)S(1)}, u32[]{:S(2)}, u32[]{:S(2)}) collective-permute-start(f32[72,512]{1,0:T(8,128)S(1)} %pad_maximum_fusion.5), channel_id=1, source_target_pairs={{0,8},{4,12},{8,0},{12,4},{1,9},{5,13},{9,1},{13,5},{2,10},{6,14},... | collective-permute-start | bytes 442376 | tf_op jit(solution)/shard_map/ppermute | solution.py:319
  321.1 7.0 %collective-permute-done.4 = f32[72,512]{1,0:T(8,128)S(1)} collective-permute-done((f32[72,512]{1,0:T(8,128)S(1)}, f32[72,512]{1,0:T(8,128)S(1)}, u32[]{:S(2)}, u32[]{:S(2)}) %collective-permute-start.4) | collective-permute-done | bytes 147488 | tf_op jit(solution)/shard_map/ppermute | solution.py:319
  328.1 3.5 collective-permute-done.5
  333.3 1.9 constant_dynamic-update-slice_fusion.6
  335.2 1.9 collective-permute-start.7
  337.2 2.3 collective-permute-done.7
  341.0 3.0 fusion.4
  344.0 3.0 fusion.5
  347.0 3.3 convolution_convert_fusion.4
  350.3 2.2 fusion.6
  352.5 2.0 pad_maximum_fusion
  (87 shorter events, 30.0 us)
Async XLA Ops:
  8.0 287.9 %all-gather.5.cloned.1.call-start = ((), (), s32[]{:S(2)}) async-start(), calls=%async_computation.1 | async-start | bytes 3145728 | tf_op jit(solution)/shard_map/all_gather | solution.py:298
  8.8 289.7 %all-gather.3.cloned.1.call-start = ((), (), s32[]{:S(2)}) async-start(), calls=%async_computation | async-start | bytes 9437184 | tf_op jit(solution)/shard_map/all_gather | solution.py:297
  9.5 322.1 %all-reduce.3.cloned.1.call-start = ((), (), s32[]{:S(2)}) async-start(), calls=%async_computation.2 | async-start | bytes 524288 | tf_op jit(solution)/shard_map/psum | solution.py:299
  12.0 5.8 %copy-start.2 = (bf16[2,2,64,256,128]{4,3,2,1,0:T(8,128)(2,1)S(1)}, bf16[2,2,64,256,128]{4,3,2,1,0:T(8,128)(2,1)}, u32[]{:S(2)}) copy-start(bf16[2,2,64,256,128]{4,3,2,1,0:T(8,128)(2,1)} %cache_ref.1) | copy-start | bytes 50331652
  243.8 3.3 copy-start.5
  243.8 4.1 %copy-start.6 = (bf16[2,4,64,4096]{3,2,1,0:T(8,128)(2,1)S(1)}, bf16[2,4,64,4096]{3,2,1,0:T(8,128)(2,1)}, u32[]{:S(2)}) copy-start(bf16[2,4,64,4096]{3,2,1,0:T(8,128)(2,1)} %param.16) | copy-start | bytes 12582916
  247.1 8.4 %collective-permute-start.9 = (bf16[2,72,2048]{2,1,0:T(8,128)(2,1)}, bf16[2,72,2048]{2,1,0:T(8,128)(2,1)}, u32[]{:S(2)}, u32[]{:S(2)}) collective-permute-start(bf16[2,72,2048]{2,1,0:T(8,128)(2,1)} %get-tuple-element.9), channel_id=1, source_target_pairs={{0,1},{1,2},{2,3},{3,0},{4,5},{5,6},{6,7},{7,4},{8,9},{9,10},{10,1... | collective-permute-start | bytes 1769480 | tf_op jit(solution)/shard_map/ppermute | solution.py:274
  248.6 3.3 copy-start.10
  250.4 3.9 %copy-start.4 = (bf16[256,2048]{1,0:T(8,128)(2,1)S(1)}, bf16[256,2048]{1,0:T(8,128)(2,1)}, u32[]{:S(2)}) copy-start(bf16[256,2048]{1,0:T(8,128)(2,1)} %param.19) | copy-start | bytes 3145732
  251.9 14.1 %collective-permute-start = (bf16[2,72,2048]{2,1,0:T(8,128)(2,1)}, bf16[2,72,2048]{2,1,0:T(8,128)(2,1)}, u32[]{:S(2)}, u32[]{:S(2)}) collective-permute-start(bf16[2,72,2048]{2,1,0:T(8,128)(2,1)} %get-tuple-element.5), channel_id=1, source_target_pairs={{0,1},{1,2},{2,3},{3,0},{4,5},{5,6},{6,7},{7,4},{8,9},{9,10},{10,1... | collective-permute-start | bytes 1769480 | tf_op jit(solution)/shard_map/ppermute | solution.py:274
  252.7 28.9 %collective-permute-start.10 = (bf16[2,72,2048]{2,1,0:T(8,128)(2,1)}, bf16[2,72,2048]{2,1,0:T(8,128)(2,1)}, u32[]{:S(2)}, u32[]{:S(2)}) collective-permute-start(bf16[2,72,2048]{2,1,0:T(8,128)(2,1)} %get-tuple-element.10), channel_id=1, source_target_pairs={{0,2},{1,3},{2,0},{3,1},{4,6},{5,7},{6,4},{7,5},{8,10},{9,11},{10,... | collective-permute-start | bytes 1769480 | tf_op jit(solution)/shard_map/ppermute | solution.py:274
  253.2 65.7 %collective-permute-start.11 = (bf16[2,72,2048]{2,1,0:T(8,128)(2,1)}, bf16[2,72,2048]{2,1,0:T(8,128)(2,1)}, u32[]{:S(2)}, u32[]{:S(2)}) collective-permute-start(bf16[2,72,2048]{2,1,0:T(8,128)(2,1)} %get-tuple-element.7), channel_id=1, source_target_pairs={{0,3},{1,0},{2,1},{3,2},{4,7},{5,4},{6,5},{7,6},{8,11},{9,8},{10,9... | collective-permute-start | bytes 1769480 | tf_op jit(solution)/shard_map/ppermute | solution.py:274
  253.9 40.0 %collective-permute-start.1 = (bf16[2,72,2048]{2,1,0:T(8,128)(2,1)}, bf16[2,72,2048]{2,1,0:T(8,128)(2,1)}, u32[]{:S(2)}, u32[]{:S(2)}) collective-permute-start(bf16[2,72,2048]{2,1,0:T(8,128)(2,1)} %get-tuple-element.6), channel_id=1, source_target_pairs={{0,2},{1,3},{2,0},{3,1},{4,6},{5,7},{6,4},{7,5},{8,10},{9,11},{10,... | collective-permute-start | bytes 1769480 | tf_op jit(solution)/shard_map/ppermute | solution.py:274
  255.5 77.8 %collective-permute-start.2 = (bf16[2,72,2048]{2,1,0:T(8,128)(2,1)}, bf16[2,72,2048]{2,1,0:T(8,128)(2,1)}, u32[]{:S(2)}, u32[]{:S(2)}) collective-permute-start(bf16[2,72,2048]{2,1,0:T(8,128)(2,1)} %get-tuple-element.3), channel_id=1, source_target_pairs={{0,3},{1,0},{2,1},{3,2},{4,7},{5,4},{6,5},{7,6},{8,11},{9,8},{10,9... | collective-permute-start | bytes 1769480 | tf_op jit(solution)/shard_map/ppermute | solution.py:274
  298.5 3.5 copy-start.8
  304.1 16.9 %collective-permute-start.3 = (f32[72,512]{1,0:T(8,128)S(1)}, f32[72,512]{1,0:T(8,128)S(1)}, u32[]{:S(2)}, u32[]{:S(2)}) collective-permute-start(f32[72,512]{1,0:T(8,128)S(1)} %pad_maximum_fusion.5), channel_id=1, source_target_pairs={{0,4},{4,8},{8,12},{12,0},{1,5},{5,9},{9,13},{13,1},{2,6},{6,10},{... | collective-permute-start | bytes 442376 | tf_op jit(solution)/shard_map/ppermute | solution.py:319
  315.1 12.9 %collective-permute-start.4 = (f32[72,512]{1,0:T(8,128)S(1)}, f32[72,512]{1,0:T(8,128)S(1)}, u32[]{:S(2)}, u32[]{:S(2)}) collective-permute-start(f32[72,512]{1,0:T(8,128)S(1)} %pad_maximum_fusion.5), channel_id=1, source_target_pairs={{0,8},{4,12},{8,0},{12,4},{1,9},{5,13},{9,1},{13,5},{2,10},{6,14},... | collective-permute-start | bytes 442376 | tf_op jit(solution)/shard_map/ppermute | solution.py:319
  318.9 12.7 %collective-permute-start.5 = (f32[72,512]{1,0:T(8,128)S(1)}, f32[72,512]{1,0:T(8,128)S(1)}, u32[]{:S(2)}, u32[]{:S(2)}) collective-permute-start(f32[72,512]{1,0:T(8,128)S(1)} %pad_maximum_fusion.5), channel_id=1, source_target_pairs={{0,12},{4,0},{8,4},{12,8},{1,13},{5,1},{9,5},{13,9},{2,14},{6,2},{... | collective-permute-start | bytes 442376 | tf_op jit(solution)/shard_map/ppermute | solution.py:319
  332.9 4.3 %collective-permute-start.6 = (bf16[72,512]{1,0:T(8,128)(2,1)S(1)}, bf16[72,512]{1,0:T(8,128)(2,1)S(1)}, u32[]{:S(2)}, u32[]{:S(2)}) collective-permute-start(bf16[72,512]{1,0:T(8,128)(2,1)S(1)} %get-tuple-element.11), channel_id=1, source_target_pairs={{0,1},{1,2},{2,3},{3,0},{4,5},{5,6},{6,7},{7,4},{8,9},{9,10},{10,1... | collective-permute-start | bytes 221192 | tf_op jit(solution)/shard_map/ppermute | solution.py:274
  335.2 4.2 %collective-permute-start.7 = (bf16[72,512]{1,0:T(8,128)(2,1)S(1)}, bf16[72,512]{1,0:T(8,128)(2,1)S(1)}, u32[]{:S(2)}, u32[]{:S(2)}) collective-permute-start(bf16[72,512]{1,0:T(8,128)(2,1)S(1)} %get-tuple-element.11), channel_id=1, source_target_pairs={{0,2},{1,3},{2,0},{3,1},{4,6},{5,7},{6,4},{7,5},{8,10},{9,11},{10,... | collective-permute-start | bytes 221192 | tf_op jit(solution)/shard_map/ppermute | solution.py:274
  337.2 3.8 %collective-permute-start.8 = (bf16[72,512]{1,0:T(8,128)(2,1)S(1)}, bf16[72,512]{1,0:T(8,128)(2,1)S(1)}, u32[]{:S(2)}, u32[]{:S(2)}) collective-permute-start(bf16[72,512]{1,0:T(8,128)(2,1)S(1)} %get-tuple-element.11), channel_id=1, source_target_pairs={{0,3},{1,0},{2,1},{3,2},{4,7},{5,4},{6,5},{7,6},{8,11},{9,8},{10,9... | collective-permute-start | bytes 221192 | tf_op jit(solution)/shard_map/ppermute | solution.py:274
  350.2 2.2 copy-start.12
  350.2 2.2 copy-start.13
  352.4 3.3 copy-start.1
  (7 other events, 12.2 us)
Sparse Core Ops, SparseCore 0:
  10.4 12.4 all-gather.4
  24.4 17.9 all-gather.2
Sparse Core Ops, SparseCore 1:
  255.5 63.4 all-reduce.2

commit v2 on v1

--- a/solution.py
+++ b/solution.py
@@ -71,9 +71,11 @@
 
 
 def project_kernel(
-    n_t, n_dp, n_sec, att_ref, w_ref, res_ref, top_ref,
+    n_t, n_dp, n_sec, att_ref, w_ref, res_ref, choose_ref, lm_ref, gram_ref,
+    top_ref, pair_ref, lm_all, pair_all, gram_all,
     held, w_vmem, acc, part, own, got,
     w_sem, local_sem, gs_sem, gr_sem, rs_sem, rr_sem,
+    lms_sem, lmr_sem, ps_sem, pr_sem, grs_sem, grr_sem, keep_sem,
 ):
     steps, rows, depth = att_ref.shape
     cols = w_ref.shape[1]
@@ -110,14 +112,66 @@
         pl.semaphore_signal(barrier, inc=1, device_id=peer(k)[1], device_id_type=MESH)
     pl.semaphore_wait(barrier, n_t - 1 + blocks - 1)
 
-    def gather(s, k):
-        return pltpu.make_async_remote_copy(
-            src_ref=att_ref.at[s],
-            dst_ref=held.at[s, t],
-            send_sem=gs_sem.at[s, k - 1],
-            recv_sem=gr_sem.at[s, k - 1],
-            device_id={"tensor": other(k)},
+    def sends(way, j):
+        return (t >= j) & (t < n_t - 1) if way == 0 else (t + j < n_t) & (t > 0)
+
+    def receives(way, j):
+        return t - 1 - j >= 0 if way == 0 else t + 1 + j < n_t
+
+    def gather(s, way, j):
+        block = lax.rem(t - j + n_t, n_t) if way == 0 else lax.rem(t + j, n_t)
+        to = lax.rem(t + 1, n_t) if way == 0 else lax.rem(t + n_t - 1, n_t)
+        return pltpu.make_async_remote_copy(
+            src_ref=att_ref.at[s] if j == 0 else held.at[s, block],
+            dst_ref=held.at[s, block],
+            send_sem=gs_sem.at[s, way, j],
+            recv_sem=gr_sem.at[s, way, j],
+            device_id={"tensor": to},
             device_id_type=MESH,
+        )
+
+    def pass_on(s):
+        for j in range(n_t - 1):
+            for way in range(2):
+
+                @pl.when(receives(way, j))
+                def _(s=s, way=way, j=j):
+                    gather(s, way, j).wait_recv()
+
+                if j + 1 < n_t - 1:
+
+                    @pl.when(sends(way, j + 1))
+                    def _(s=s, way=way, j=j):
+                        gather(s, way, j + 1).start()
+
+    width = lm_all.shape[-1]
+    chosen = choose_ref.shape[1]
+
+    def columns(b):
+        return pl.ds(pl.multiple_of(lax.rem(b, n_sec) * width, width), width)
+
+    def send_lm(k):
+        b, to = peer(k)
+        return pltpu.make_async_remote_copy(
+            src_ref=lm_ref.at[:, :, columns(b)], dst_ref=lm_all.at[me],
+            send_sem=lms_sem.at[k - 1], recv_sem=lmr_sem.at[k - 1],
+            device_id=to, device_id_type=MESH,
+        )
+
+    def send_pair(a, s, k):
+        b, to = peer(k)
+        at = pl.ds(s * chosen, chosen)
+        return pltpu.make_async_remote_copy(
+            src_ref=pair_ref.at[a, at, columns(b)], dst_ref=pair_all.at[me, a, at],
+            send_sem=ps_sem.at[a, s, k - 1], recv_sem=pr_sem.at[a, s, k - 1],
+            device_id=to, device_id_type=MESH,
+        )
+
+    def send_gram(k):
+        return pltpu.make_async_remote_copy(
+            src_ref=gram_ref, dst_ref=gram_all.at[t],
+            send_sem=grs_sem.at[k - 1], recv_sem=grr_sem.at[k - 1],
+            device_id={"tensor": other(k)}, device_id_type=MESH,
         )
 
     def scatter(s, h, k):
@@ -131,8 +185,11 @@
         )
 
     def start_gather(s):
-        for k in range(n_t - 1, 0, -1):
-            gather(s, k).start()
+        for way in range(2):
+
+            @pl.when(sends(way, 0))
+            def _(s=s, way=way):
+                gather(s, way, 0).start()
 
     def finish(s):
         for h in range(halves):
@@ -143,7 +200,16 @@
                 total = own[s % 2, :, at] + res_ref[s, :, at].astype(F32)
                 for k in range(1, blocks):
                     total += got[s, h, k - 1, :, pl.ds(c, tile)].astype(F32)
-                top_ref[s, :, at] = total.astype(BF16)
+                total = total.astype(BF16)
+                top_ref[s, :, at] = total
+                for a, at_step in ((0, s), (1, s - 1)):
+                    if 0 <= at_step < steps - 1:
+                        picked = jnp.dot(choose_ref[at_step], total, preferred_element_type=F32)
+                        pair_ref[a, pl.ds(at_step * chosen, chosen), at] = picked.astype(BF16)
+        for a, at_step in ((0, s), (1, s - 1)):
+            if 0 <= at_step < steps - 1:
+                for k in range(1, blocks):
+                    send_pair(a, at_step, k).start()
 
     start_gather(0)
     for c in locals_:
@@ -152,11 +218,20 @@
         c.start()
     if steps > 1:
         start_gather(1)
+    for k in range(1, blocks):
+        send_lm(k).start()
+    for k in range(1, n_t):
+        send_gram(k).start()
+    keeps = [
+        pltpu.make_async_copy(lm_ref.at[:, :, columns(me)], lm_all.at[me], keep_sem.at[0]),
+        pltpu.make_async_copy(gram_ref, gram_all.at[t], keep_sem.at[1]),
+    ]
+    for c in keeps:
+        c.start()
     for c in locals_:
         c.wait()
     for s in range(steps):
-        for k in range(1, n_t):
-            gather(s, k).wait_recv()
+        pass_on(s)
         if s + 2 < steps:
             start_gather(s + 2)
         if s == 0:
@@ -192,36 +267,187 @@
         for h in range(halves):
             for k in range(1, blocks):
                 scatter(s, h, k).wait_send()
+    last = pltpu.make_async_copy(pair_ref.at[:, :, columns(me)], pair_all.at[me], keep_sem.at[2])
+    last.start()
     for s in range(steps):
-        for k in range(1, n_t):
-            gather(s, k).wait_send()
-
-
-def project(mesh_shape, attended, w_out, residual):
+        for way in range(2):
+            for j in range(n_t - 1):
+
+                @pl.when(sends(way, j))
+                def _(s=s, way=way, j=j):
+                    gather(s, way, j).wait_send()
+
+    for k in range(1, blocks):
+        send_lm(k).wait()
+    for k in range(1, n_t):
+        send_gram(k).wait()
+    for s in range(steps - 1):
+        for a in range(2):
+            for k in range(1, blocks):
+                send_pair(a, s, k).wait()
+    for c in keeps + [last]:
+        c.wait()
+
+
+def train_kernel(
+    n_t, n_dp, n_sec, scale, pair_ref, lm_ref, down_ref, up_all, up_ref, gram_all, lm_all, pair_all,
+    grad_down_ref, grad_up_ref,
+    down, ups, gsum, gram_got, both, both_all, inner, inner_all, lms, pairs,
+    in_sem, gs_sem, gr_sem, bs_sem, br_sem, is_sem, ir_sem,
+):
+    blocks = n_dp * n_sec
+    count = pair_ref.shape[1]
+    rank_width = up_ref.shape[0]
+    width = up_ref.shape[1]
+    t = lax.axis_index("tensor")
+    section = lax.axis_index("section")
+    me = lax.axis_index("dp") * n_sec + section
+
+    loads = [
+        pltpu.make_async_copy(up_all, ups, in_sem.at[0]),
+        pltpu.make_async_copy(down_ref, down, in_sem.at[1]),
+        pltpu.make_async_copy(lm_all, lms, in_sem.at[2]),
+        pltpu.make_async_copy(pair_all, pairs, in_sem.at[3]),
+    ]
+    for c in loads:
+        c.start()
+
+    def peer(k):
+        b = lax.rem(me + k, blocks)
+        return {"dp": b // n_sec, "section": lax.rem(b, n_sec)}
+
+    barrier = pltpu.get_barrier_semaphore()
+    for k in range(1, n_t):
+        pl.semaphore_signal(
+            barrier, inc=1, device_id={"tensor": lax.rem(t + k, n_t)}, device_id_type=MESH
+        )
+    for k in range(1, blocks):
+        pl.semaphore_signal(barrier, inc=1, device_id=peer(k), device_id_type=MESH)
+    pl.semaphore_wait(barrier, n_t - 1 + blocks - 1)
+
+    def send_gram(k):
+        return pltpu.make_async_remote_copy(
+            src_ref=gsum, dst_ref=gram_got.at[section],
+            send_sem=gs_sem.at[k - 1], recv_sem=gr_sem.at[k - 1],
+            device_id={"section": lax.rem(section + k, n_sec)}, device_id_type=MESH,
+        )
+
+    def send_both(k):
+        return pltpu.make_async_remote_copy(
+            src_ref=both, dst_ref=both_all.at[t],
+            send_sem=bs_sem.at[k - 1], recv_sem=br_sem.at[k - 1],
+            device_id={"tensor": lax.rem(t + k, n_t)}, device_id_type=MESH,
+        )
+
+    def send_inner(k):
+        return pltpu.make_async_remote_copy(
+            src_ref=inner, dst_ref=inner_all.at[me],
+            send_sem=is_sem.at[k - 1], recv_sem=ir_sem.at[k - 1],
+            device_id=peer(k), device_id_type=MESH,
+        )
+
+    gsum[...] = sum(gram_all[i] for i in range(n_t))
+    gram_got[section] = gsum[...]
+    for k in range(1, n_sec):
+        send_gram(k).start()
+    loads[0].wait()
+    both[:, rank_width:] = lax.dot_general(
+        pair_ref[1], ups[...], (((1,), (1,)), ((), ())), preferred_element_type=F32
+    )
+    loads[1].wait()
+    pre = jnp.dot(pair_ref[0], down[2], preferred_element_type=F32)
+    for c in range(2):
+        pre += jnp.dot(lm_ref[c], down[c], preferred_element_type=F32)
+    both[:, :rank_width] = pre
+    both_all[t] = both[...]
+    for k in range(1, n_t):
+        send_both(k).start()
+    for k in range(1, n_sec):
+        send_gram(k).wait()
+    for k in range(1, n_t):
+        send_both(k).wait()
+    total = both_all[0]
+    for i in range(1, n_t):
+        total += both_all[i]
+    gram = gram_got[0]
+    for i in range(1, n_sec):
+        gram += gram_got[i]
+    pre, goal = total[:, :rank_width], total[:, rank_width:]
+    sigma = jax.nn.sigmoid(pre)
+    gated = (pre * sigma).astype(BF16)
+    back = jnp.dot(
+        gated.astype(F32), gram, precision=lax.Precision.HIGHEST, preferred_element_type=F32
+    ) - goal
+    back = back / scale
+    inner[:, :rank_width] = gated
+    inner[:, rank_width:] = (back * sigma * (1.0 + pre * (1.0 - sigma))).astype(BF16)
+    inner_all[me] = inner[...]
+    for k in range(1, blocks):
+        send_inner(k).start()
+    loads[2].wait()
+    loads[3].wait()
+    for k in range(1, blocks):
+        send_inner(k).wait()
+    rows = blocks * count
+    gated = inner_all[:, :, :rank_width].reshape(rows, rank_width)
+    dpre = inner_all[:, :, rank_width:].reshape(rows, rank_width)
+    tile = min(512, width)
+
+    def body(i, _):
+        at = pl.ds(pl.multiple_of(i * tile, tile), tile)
+        over = (((0,), (0,)), ((), ()))
+        pred = jnp.dot(gated, up_ref[:, at], preferred_element_type=F32)
+        target = pairs[:, 1, :, at].reshape(rows, tile).astype(F32)
+        cotangent = ((pred - target) / scale).astype(BF16)
+        grad_up_ref[:, at] = lax.dot_general(
+            gated, cotangent, over, preferred_element_type=F32
+        ).astype(BF16)
+        for c in range(3):
+            x = lms[:, c, :, at] if c < 2 else pairs[:, 0, :, at]
+            grad_down_ref[c, at, :] = lax.dot_general(
+                x.reshape(rows, tile), dpre, over, preferred_element_type=F32
+            ).astype(BF16)
+        return 0
+
+    lax.fori_loop(0, width // tile, body, 0)
+
+
+def fits(mesh_shape, attended, w_out, residual):
+    blocks = mesh_shape["dp"] * mesh_shape["section"]
+    whole = attended.shape[1] % 16 == 0 and residual.shape[1] % 32 == 0
+    return whole and w_out.shape[1] % 1024 == 0 and mesh_shape["tensor"] > 1 and blocks > 1
+
+
+def project_plain(attended, w_out, residual):
+    whole = lax.all_gather(attended, "tensor", axis=1, tiled=True)
+    partial_rows = jnp.einsum("srj,jk->srk", whole, w_out, preferred_element_type=F32)
+    summed = lax.psum_scatter(partial_rows, ("dp", "section"), scatter_dimension=1, tiled=True)
+    return (residual.astype(F32) + summed).astype(BF16)
+
+
+def project(mesh_shape, attended, w_out, residual, choose, low_mid, gram):
     steps, rows, depth = attended.shape
     cols = w_out.shape[1]
     n_t, n_dp, n_sec = mesh_shape["tensor"], mesh_shape["dp"], mesh_shape["section"]
     blocks = n_dp * n_sec
     owned = residual.shape[1]
-    if rows % 16 or owned % 16 or cols % 1024 or n_t < 2 or blocks < 2:
-        whole = lax.all_gather(attended, "tensor", axis=1, tiled=True)
-        partial_rows = jnp.einsum("srj,jk->srk", whole, w_out, preferred_element_type=F32)
-        summed = lax.psum_scatter(
-            partial_rows, ("dp", "section"), scatter_dimension=1, tiled=True
-        )
-        return (residual.astype(F32) + summed).astype(BF16)
+    count = low_mid.shape[1]
     halves = 2
     half = cols // halves
     dma = pltpu.SemaphoreType.DMA
+    hbm, vmem = pl.BlockSpec(memory_space=pl.ANY), pl.BlockSpec(memory_space=pltpu.VMEM)
+    spread = jax.ShapeDtypeStruct((blocks, 2, count, cols // n_sec), BF16)
     return pl.pallas_call(
         functools.partial(project_kernel, n_t, n_dp, n_sec),
-        out_shape=jax.ShapeDtypeStruct(residual.shape, BF16),
-        in_specs=[
-            pl.BlockSpec(memory_space=pl.ANY),
-            pl.BlockSpec(memory_space=pl.ANY),
-            pl.BlockSpec(memory_space=pltpu.VMEM),
-        ],
-        out_specs=pl.BlockSpec(memory_space=pltpu.VMEM),
+        out_shape=(
+            jax.ShapeDtypeStruct(residual.shape, BF16),
+            jax.ShapeDtypeStruct((2, count, cols), BF16),
+            spread,
+            spread,
+            jax.ShapeDtypeStruct((n_t,) + gram.shape, F32),
+        ),
+        in_specs=[hbm, hbm, vmem, vmem, hbm, hbm],
+        out_specs=(vmem, vmem, hbm, hbm, hbm),
         scratch_shapes=[
             pltpu.VMEM((steps, n_t, rows, depth), BF16),
             pltpu.VMEM((depth, cols), BF16),
@@ -231,20 +457,68 @@
             pltpu.VMEM((steps, halves, blocks - 1, owned, half), BF16),
             dma((halves,)),
             dma((steps,)),
-            dma((steps, n_t - 1)),
-            dma((steps, n_t - 1)),
+            dma((steps, 2, n_t - 1)),
+            dma((steps, 2, n_t - 1)),
             dma((steps, halves, blocks - 1)),
             dma((steps, halves, blocks - 1)),
+            dma((blocks - 1,)),
+            dma((blocks - 1,)),
+            dma((2, steps - 1, blocks - 1)),
+            dma((2, steps - 1, blocks - 1)),
+            dma((n_t - 1,)),
+            dma((n_t - 1,)),
+            dma((3,)),
         ],
         compiler_params=pltpu.CompilerParams(
-            collective_id=0, has_side_effects=True, vmem_limit_bytes=61 * 2**20
+            collective_id=0, has_side_effects=True, vmem_limit_bytes=62 * 2**20
         ),
         cost_estimate=pl.CostEstimate(
             flops=2 * steps * rows * n_t * depth * cols,
             bytes_accessed=2 * w_out.size,
             transcendentals=0,
         ),
-    )(attended, w_out, residual)
+    )(attended, w_out, residual, choose, low_mid, gram)
+
+
+def train(mesh_shape, scale, pair, low_mid, down_full, up_full, up_map, gram_all, lm_all, pair_all):
+    n_t, n_dp, n_sec = mesh_shape["tensor"], mesh_shape["dp"], mesh_shape["section"]
+    blocks = n_dp * n_sec
+    count = pair.shape[1]
+    rank_width, width = up_map.shape
+    dma = pltpu.SemaphoreType.DMA
+    hbm, vmem = pl.BlockSpec(memory_space=pl.ANY), pl.BlockSpec(memory_space=pltpu.VMEM)
+    square = (rank_width, rank_width)
+    return pl.pallas_call(
+        functools.partial(train_kernel, n_t, n_dp, n_sec, scale),
+        out_shape=(
+            jax.ShapeDtypeStruct((3, width, rank_width), BF16),
+            jax.ShapeDtypeStruct((rank_width, width), BF16),
+        ),
+        in_specs=[vmem, vmem, hbm, hbm, vmem, vmem, hbm, hbm],
+        out_specs=(vmem, vmem),
+        scratch_shapes=[
+            pltpu.VMEM(down_full.shape, BF16),
+            pltpu.VMEM(up_full.shape, BF16),
+            pltpu.VMEM(square, F32),
+            pltpu.VMEM((n_sec,) + square, F32),
+            pltpu.VMEM((count, 2 * rank_width), F32),
+            pltpu.VMEM((n_t, count, 2 * rank_width), F32),
+            pltpu.VMEM((count, 2 * rank_width), BF16),
+            pltpu.VMEM((blocks, count, 2 * rank_width), BF16),
+            pltpu.VMEM(lm_all.shape, BF16),
+            pltpu.VMEM(pair_all.shape, BF16),
+            dma((4,)),
+            dma((max(1, n_sec - 1),)),
+            dma((max(1, n_sec - 1),)),
+            dma((n_t - 1,)),
+            dma((n_t - 1,)),
+            dma((blocks - 1,)),
+            dma((blocks - 1,)),
+        ],
+        compiler_params=pltpu.CompilerParams(
+            collective_id=1, has_side_effects=True, vmem_limit_bytes=48 * 2**20
+        ),
+    )(pair, low_mid, down_full, up_full, up_map, gram_all, lm_all, pair_all)
 
 
 def on_device(
@@ -258,7 +532,8 @@
     rank_width = up_map.shape[0]
     col_width = up_map.shape[1]
 
-    most = min(MOST, owned)
+    kernels = fits(mesh_shape, queries, w_out, residual)
+    most = 32 if kernels else min(MOST, owned)
     mine = lax.dynamic_slice_in_dim(accepted, section * owned, owned, axis=1)[: steps - 1]
     place = jnp.cumsum(mine, axis=1) - 1
     choose = (place[:, None, :] == jnp.arange(most)[None, :, None]) & (mine[:, None, :] > 0)
@@ -291,18 +566,27 @@
             laid = lax.dynamic_update_slice_in_dim(laid, piece, b * size, axis=axis)
         return laid
 
+    down_full = lax.all_gather(down_map, "section", axis=1, tiled=True)
+    up_full = lax.all_gather(up_map, "section", axis=1, tiled=True)
+    gram = jnp.einsum("kj,lj->kl", up_map, up_map, preferred_element_type=F32)
+    attended = attend(queries, cache, fresh_kv, lengths)
+    if kernels:
+        top_hidden, pair, lm_all, pair_all, gram_all = project(
+            mesh_shape, attended, w_out, residual, choose, low_mid, gram
+        )
+        grad_down, grad_up = train(
+            mesh_shape, steps - 1, pair, low_mid, down_full, up_full, up_map,
+            gram_all, lm_all, pair_all,
+        )
+        return top_hidden, grad_down, grad_up
+
     low_mid_all = in_order(
         [half_for(low_mid, 0)] + [swap(half_for(low_mid, k), k) for k in range(1, blocks)]
     )
-    down_full = lax.all_gather(down_map, "section", axis=1, tiled=True)
-    up_full = lax.all_gather(up_map, "section", axis=1, tiled=True)
-    gram = lax.psum(
-        jnp.einsum("kj,lj->kl", up_map, up_map, preferred_element_type=F32), ("tensor", "section")
-    )
+    gram = lax.psum(gram, ("tensor", "section"))
     pre_early = jnp.einsum("cnj,cjk->nk", low_mid, down_full[:2], preferred_element_type=F32)
 
-    attended = attend(queries, cache, fresh_kv, lengths)
-    top_hidden = project(mesh_shape, attended, w_out, residual)
+    top_hidden = project_plain(attended, w_out, residual)
 
     top = compact(top_hidden[: steps - 1])
     target = compact(top_hidden[1:])

time: 364 us -> 321 us (0.88)
  Pallas kernels: 221 us -> 276 us
  waiting for transfers between devices: 47.3 us -> 1.42 us
  starting transfers between devices: 20.7 us -> 0.08 us
  matrix products: 24.8 us -> 4.71 us
  local copies, waits for them, and re-layouts: 27.8 us -> 21.7 us
    pallas_call x0 -> x1, Pallas kernels: none -> 63.8 us  [train(): pl.pallas_call(functools.partial(train_kernel, n_t, n_dp, n_sec, scale),...]
    ppermute x12 -> x0, waiting for transfers between devices: 45.9 us -> none  [the longest x9 35.2 us: swap(): return lax.ppermute(x, ('dp', 'section'), pairs)]
    dot_general x9 -> x1, matrix products: 22 us -> 1.17 us  [on_device(): gram = jnp.einsum('kj,lj->kl', up_map, up_map, preferred_element_type=F32)]
    ppermute x12 -> x0, starting transfers between devices: 20.6 us -> none  [the longest x3 14.7 us: on_device(): total = total + lax.ppermute(both, 'tensor', pairs)]
    dynamic_update_slice x9 -> x0, local copies, waits for them, and re-layouts: 11.7 us -> none  [in_order(): laid = lax.dynamic_update_slice_in_dim(laid, piece, b * size, axis=axis)]
    pallas_call x1, Pallas kernels: 206 us -> 197 us  [project(): pl.pallas_call(functools.partial(project_kernel, n_t, n_dp, n_sec), out_s...]
    unnamed x35 -> x27, local copies, waits for them, and re-layouts: 9.13 us -> 14.8 us
  transfers between devices with their start and end apart: 15 -> 2, of which waited for: 8 -> 0; matrix products, arithmetic and copies ran while one was open for 10% -> 5% of each run, Pallas kernels for 61% -> 66%
where the time goes in v2:
time: 321 us; the launch traced here: 320 us
  Pallas kernels  276 us (86%)
  local copies, waits for them, and re-layouts  21.7 us (7%)
  between operations  14.2 us (4%)
  matrix products  4.71 us (1%)
    pallas_call x1, Pallas kernels, project(): pl.pallas_call(functools.partial(project_kernel, n_t, n_dp, n_sec), out_s...  197 us
    pallas_call x1, Pallas kernels, train(): pl.pallas_call(functools.partial(train_kernel, n_t, n_dp, n_sec, scale),...  63.8 us
    pallas_call x1, Pallas kernels, attend(): pl.pallas_call(functools.partial(attend_kernel, group), grid=(kv, rows //...  15.2 us
    unnamed x27, local copies, waits for them, and re-layouts  14.8 us
  transfers between devices with their start and end apart: 2, of which 0 were waited for; matrix products, arithmetic and copies ran while one was open for 5% of the time, Pallas kernels for 66%

profile of v2, /device:TPU:9, one launch (start us, length us, event | category | flops | bytes accessed | tf_op | source)
XLA Modules:
  0.0 320.2 jit_solution(14431844185669183432)
XLA Ops:
  7.2 0.7 all-gather.5.cloned.1.call-update
  8.0 0.7 all-gather.3.cloned.1.call-update
  8.8 0.5 copy.16
  9.3 0.6 copy.13
  9.9 0.3 copy-done.9
  10.2 0.2 copy.20
  10.8 5.8 %copy-done.3 = bf16[2,2,64,256,128]{4,3,2,1,0:T(8,128)(2,1)S(1)} copy-done((bf16[2,2,64,256,128]{4,3,2,1,0:T(8,128)(2,1)S(1)}, bf16[2,2,64,256,128]{4,3,2,1,0:T(8,128)(2,1)}, u32[]{:S(2)}) %copy-start.3) | copy-done | bytes 16777240
  16.5 15.2 %shard_map.121 = bf16[64,2,64,128]{3,2,1,0:T(8,128)(2,1)S(1)} custom-call(bf16[64,2,64,128]{3,2,1,0:T(8,128)(2,1)S(1)} %bitcast.27, bf16[2,2,64,256,128]{4,3,2,1,0:T(8,128)(2,1)S(1)} %copy-done.3, bf16[2,2,64,16,128]{4,3,2,1,0:T(8,128)(2,1)S(1)} %pad.4.fresh_ref, f32[64,1,256]{2,1,0:T(1,128)S(1)} %compare_select_fusion.bias_ref), custom_call_target="tpu_custom_call" | custom-call | flops 1073741824 | bytes 20971520 | tf_op jit(solution)/shard_map/pallas_call | solution.py:51
  31.7 1.7 copy.19
  33.4 4.4 %reshape.65.att_ref = bf16[4,64,4096]{2,1,0:T(8,128)(2,1)} reshape(bf16[4,64,2,16,128]{4,3,2,1,0:T(8,128)(2,1)} %bitcast.29) | data formatting | bytes 4194304 | tf_op jit(solution)/shard_map/reshape | solution.py:70
  37.9 0.2 reduce_window_sum.11
  38.1 0.6 fusion.7.choose_ref
  38.7 1.2 fusion.12.gram_ref
  39.9 1.8 convolution_convert_fusion
  41.7 1.8 convolution_convert_fusion.1
  43.5 1.3 pad_maximum_fusion.lm_ref
  44.7 196.8 %shard_map.122 = (bf16[4,64,4096]{2,1,0:T(8,128)(2,1)}, bf16[2,96,4096]{2,1,0:T(8,128)(2,1)}, bf16[4,2,96,2048]{3,2,1,0:T(8,128)(2,1)}, bf16[4,2,96,2048]{3,2,1,0:T(8,128)(2,1)}, f32[4,256,256]{2,1,0:T(8,128)}) custom-call(bf16[4,64,4096]{2,1,0:T(8,128)(2,1)} %reshape.65.att_ref, bf16[4096,4096]{1,0:T(8,128)(2,1)} %w_ref.1, bf16[4,64,4096]{2,1,0:T(8,128)(2,1)} %res_ref.1, ...), custom_call_target="tpu_custom_call" | custom-call | flops 34359738368 | bytes 33554432 | tf_op jit(solution)/shard_map/pallas_call | solution.py:440
  241.6 1.4 copy-done.4
  243.0 1.2 copy-done.5
  244.2 63.8 %shard_map.123 = (bf16[3,2048,256]{2,1,0:T(8,128)(2,1)}, bf16[256,2048]{1,0:T(8,128)(2,1)S(1)}) custom-call(bf16[2,96,4096]{2,1,0:T(8,128)(2,1)S(1)} %copy-done.4, bf16[2,96,4096]{2,1,0:T(8,128)(2,1)} %pad_maximum_fusion.lm_ref, bf16[3,4096,256]{2,1,0:T(8,128)(2,1)} %all-gather.3.cloned.1.call-done.down_ref, ...), custom_call_target="tpu_custom_call" | custom-call | tf_op jit(solution)/shard_map/pallas_call | solution.py:491
  308.1 1.3 copy.24
  309.4 1.3 copy-done.6
  310.7 1.7 copy.25
  312.4 1.0 copy.26
  (26 shorter events, 0.6 us)
Async XLA Ops:
  7.2 30.6 %copy-start = (s32[4,128]{1,0:T(4,128)S(1)}, s32[4,128]{1,0:T(4,128)}, u32[]{:S(2)}) copy-start(s32[4,128]{1,0:T(4,128)} %param.17) | copy-start | bytes 6148
  7.2 1.6 copy-start.7
  7.2 234.4 %all-gather.5.cloned.1.call-start = ((), (), s32[]{:S(2)}) async-start(), calls=%async_computation.1 | async-start | bytes 3145728 | tf_op jit(solution)/shard_map/all_gather | solution.py:570
  7.9 233.7 %all-gather.3.cloned.1.call-start = ((), (), s32[]{:S(2)}) async-start(), calls=%async_computation | async-start | bytes 9437184 | tf_op jit(solution)/shard_map/all_gather | solution.py:569
  9.3 1.0 copy-start.9
  9.3 1.3 copy-start.10
  10.7 5.8 %copy-start.3 = (bf16[2,2,64,256,128]{4,3,2,1,0:T(8,128)(2,1)S(1)}, bf16[2,2,64,256,128]{4,3,2,1,0:T(8,128)(2,1)}, u32[]{:S(2)}) copy-start(bf16[2,2,64,256,128]{4,3,2,1,0:T(8,128)(2,1)} %cache_ref.1) | copy-start | bytes 50331652
  33.4 5.3 %copy-start.2 = (bf16[256,2048]{1,0:T(8,128)(2,1)S(1)}, bf16[256,2048]{1,0:T(8,128)(2,1)}, u32[]{:S(2)}) copy-start(bf16[256,2048]{1,0:T(8,128)(2,1)} %up_ref.1) | copy-start | bytes 3145732
  241.6 1.4 copy-start.4
  243.0 1.2 copy-start.5
  244.2 63.9 %copy-start.8 = (bf16[4,64,4096]{2,1,0:T(8,128)(2,1)S(1)}, bf16[4,64,4096]{2,1,0:T(8,128)(2,1)}, u32[]{:S(2)}) copy-start(bf16[4,64,4096]{2,1,0:T(8,128)(2,1)} %get-tuple-element.20) | copy-start | bytes 6291460
  308.1 2.6 copy-start.6
  310.7 2.6 copy-start.1
Sparse Core Ops, SparseCore 0:
  9.6 12.4 all-gather.4
  23.6 17.9 all-gather.2

commit v3 on v2

--- a/solution.py
+++ b/solution.py
@@ -71,20 +71,23 @@
 
 
 def project_kernel(
-    n_t, n_dp, n_sec, att_ref, w_ref, res_ref, choose_ref, lm_ref, gram_ref,
-    top_ref, pair_ref, lm_all, pair_all, gram_all,
-    held, w_vmem, acc, part, own, got,
-    w_sem, local_sem, gs_sem, gr_sem, rs_sem, rr_sem,
-    lms_sem, lmr_sem, ps_sem, pr_sem, grs_sem, grr_sem, keep_sem,
+    n_t, n_dp, n_sec, att_ref, w_ref, res_ref, choose_ref, lm_ref,
+    top_ref, pair_ref, lm_all, pair_all,
+    held, w_vmem, acc, part, own, got, part_dp, got_dp,
+    w_sem, local_sem, gs_sem, gr_sem, rs_sem, rr_sem, ds_sem, dr_sem,
+    lms_sem, lmr_sem, ps_sem, pr_sem, keep_sem,
 ):
     steps, rows, depth = att_ref.shape
     cols = w_ref.shape[1]
     blocks = n_dp * n_sec
     owned = res_ref.shape[1]
-    halves, half = got.shape[1], got.shape[4]
+    halves, half = got.shape[1], got.shape[5]
     tile = 512
+    ahead = 3
+    pieces = gs_sem.shape[3]
     t = lax.axis_index("tensor")
-    me = lax.axis_index("dp") * n_sec + lax.axis_index("section")
+    d, sec = lax.axis_index("dp"), lax.axis_index("section")
+    me = d * n_sec + sec
 
     w_copies = [
         pltpu.make_async_copy(
@@ -118,31 +121,33 @@
     def receives(way, j):
         return t - 1 - j >= 0 if way == 0 else t + 1 + j < n_t
 
-    def gather(s, way, j):
+    def gather(s, way, j, p):
+        at = pl.ds(p * (rows // pieces), rows // pieces)
         block = lax.rem(t - j + n_t, n_t) if way == 0 else lax.rem(t + j, n_t)
         to = lax.rem(t + 1, n_t) if way == 0 else lax.rem(t + n_t - 1, n_t)
         return pltpu.make_async_remote_copy(
-            src_ref=att_ref.at[s] if j == 0 else held.at[s, block],
-            dst_ref=held.at[s, block],
-            send_sem=gs_sem.at[s, way, j],
-            recv_sem=gr_sem.at[s, way, j],
+            src_ref=att_ref.at[s, at] if j == 0 else held.at[s, block, at],
+            dst_ref=held.at[s, block, at],
+            send_sem=gs_sem.at[s, way, j, p],
+            recv_sem=gr_sem.at[s, way, j, p],
             device_id={"tensor": to},
             device_id_type=MESH,
         )
 
-    def pass_on(s):
-        for j in range(n_t - 1):
-            for way in range(2):
-
-                @pl.when(receives(way, j))
-                def _(s=s, way=way, j=j):
-                    gather(s, way, j).wait_recv()
-
-                if j + 1 < n_t - 1:
-
-                    @pl.when(sends(way, j + 1))
-                    def _(s=s, way=way, j=j):
-                        gather(s, way, j + 1).start()
+    def pass_on(s, hops):
+        for j in hops:
+            for p in range(pieces):
+                for way in range(2):
+
+                    @pl.when(receives(way, j))
+                    def _(s=s, way=way, j=j, p=p):
+                        gather(s, way, j, p).wait_recv()
+
+                    if j + 1 < n_t - 1:
+
+                        @pl.when(sends(way, j + 1))
+                        def _(s=s, way=way, j=j, p=p):
+                            gather(s, way, j + 1, p).start()
 
     width = lm_all.shape[-1]
     chosen = choose_ref.shape[1]
@@ -167,39 +172,70 @@
             device_id=to, device_id_type=MESH,
         )
 
-    def send_gram(k):
+    def rows_of(i, q):
+        b = lax.rem(d + i, n_dp) * n_sec + lax.rem(sec + q, n_sec)
+        return pl.ds(pl.multiple_of(b * owned, owned), owned)
+
+    def to_section(s, h, q):
         return pltpu.make_async_remote_copy(
-            src_ref=gram_ref, dst_ref=gram_all.at[t],
-            send_sem=grs_sem.at[k - 1], recv_sem=grr_sem.at[k - 1],
-            device_id={"tensor": other(k)}, device_id_type=MESH,
-        )
-
-    def scatter(s, h, k):
+            src_ref=part.at[s % 2, h, q - 1],
+            dst_ref=got.at[s, h, q - 1],
+            send_sem=rs_sem.at[s, h, q - 1],
+            recv_sem=rr_sem.at[s, h, q - 1],
+            device_id={"section": lax.rem(sec + q, n_sec)},
+            device_id_type=MESH,
+        )
+
+    def to_dp(s, h, i):
         return pltpu.make_async_remote_copy(
-            src_ref=part.at[s % 2, h, k - 1],
-            dst_ref=got.at[s, h, k - 1],
-            send_sem=rs_sem.at[s, h, k - 1],
-            recv_sem=rr_sem.at[s, h, k - 1],
-            device_id=peer(k)[1],
+            src_ref=part_dp.at[s % 2, h, i - 1],
+            dst_ref=got_dp.at[s, h, i - 1],
+            send_sem=ds_sem.at[s, h, i - 1],
+            recv_sem=dr_sem.at[s, h, i - 1],
+            device_id={"dp": lax.rem(d + i, n_dp)},
             device_id_type=MESH,
         )
+
+    def add_sections(s, h):
+        for q in range(1, n_sec):
+            to_section(s, h, q).wait_recv()
+        for c in range(0, half, tile):
+            at, wide = pl.ds(c, tile), pl.ds(h * half + c, tile)
+            for i in range(n_dp):
+                total = own[s % 2, i, :, wide]
+                for q in range(1, n_sec):
+                    total += got[s, h, q - 1, i, :, at].astype(F32)
+                if i == 0:
+                    own[s % 2, 0, :, wide] = total
+                else:
+                    part_dp[s % 2, h, i - 1, :, at] = total.astype(BF16)
+        for i in range(1, n_dp):
+            to_dp(s, h, i).start()
+
+    def wait_sent(s):
+        for h in range(halves):
+            for q in range(1, n_sec):
+                to_section(s, h, q).wait_send()
+            for i in range(1, n_dp):
+                to_dp(s, h, i).wait_send()
 
     def start_gather(s):
         for way in range(2):
 
             @pl.when(sends(way, 0))
             def _(s=s, way=way):
-                gather(s, way, 0).start()
+                for p in range(pieces):
+                    gather(s, way, 0, p).start()
 
     def finish(s):
         for h in range(halves):
-            for k in range(1, blocks):
-                scatter(s, h, k).wait_recv()
+            for i in range(1, n_dp):
+                to_dp(s, h, i).wait_recv()
             for c in range(0, half, tile):
                 at = pl.ds(h * half + c, tile)
-                total = own[s % 2, :, at] + res_ref[s, :, at].astype(F32)
-                for k in range(1, blocks):
-                    total += got[s, h, k - 1, :, pl.ds(c, tile)].astype(F32)
+                total = own[s % 2, 0, :, at] + res_ref[s, :, at].astype(F32)
+                for i in range(1, n_dp):
+                    total += got_dp[s, h, i - 1, :, pl.ds(c, tile)].astype(F32)
                 total = total.astype(BF16)
                 top_ref[s, :, at] = total
                 for a, at_step in ((0, s), (1, s - 1)):
@@ -216,31 +252,24 @@
         c.start()
     for c in w_copies:
         c.start()
-    if steps > 1:
-        start_gather(1)
+    for s in range(1, min(ahead, steps)):
+        start_gather(s)
     for k in range(1, blocks):
         send_lm(k).start()
-    for k in range(1, n_t):
-        send_gram(k).start()
-    keeps = [
-        pltpu.make_async_copy(lm_ref.at[:, :, columns(me)], lm_all.at[me], keep_sem.at[0]),
-        pltpu.make_async_copy(gram_ref, gram_all.at[t], keep_sem.at[1]),
-    ]
+    keeps = [pltpu.make_async_copy(lm_ref.at[:, :, columns(me)], lm_all.at[me], keep_sem.at[0])]
     for c in keeps:
         c.start()
     for c in locals_:
         c.wait()
     for s in range(steps):
-        pass_on(s)
-        if s + 2 < steps:
-            start_gather(s + 2)
+        pass_on(s, range(0 if s == 0 else 1, n_t - 1))
+        if s + ahead < steps:
+            start_gather(s + ahead)
         if s == 0:
             for c in w_copies:
                 c.wait()
         if s >= 2:
-            for h in range(halves):
-                for k in range(1, blocks):
-                    scatter(s - 2, h, k).wait_send()
+            wait_sent(s - 2)
         for h in range(halves):
 
             def body(i, _, s=s, h=h):
@@ -249,25 +278,26 @@
                 lhs = held[s].reshape(n_t * rows, depth)
                 prod = jnp.dot(lhs, w_vmem[:, wide], preferred_element_type=F32)
                 acc[...] = prod
-                own[s % 2, :, wide] = acc[pl.ds(pl.multiple_of(me * owned, owned), owned), :]
-                for k in range(1, blocks):
-                    b = peer(k)[0]
-                    part[s % 2, h, k - 1, :, at] = acc[
-                        pl.ds(pl.multiple_of(b * owned, owned), owned), :
-                    ].astype(BF16)
+                for i in range(n_dp):
+                    own[s % 2, i, :, wide] = acc[rows_of(i, 0), :]
+                    for q in range(1, n_sec):
+                        part[s % 2, h, q - 1, i, :, at] = acc[rows_of(i, q), :].astype(BF16)
                 return 0
 
             lax.fori_loop(0, half // tile, body, 0)
-            for k in range(1, blocks):
-                scatter(s, h, k).start()
+            for q in range(1, n_sec):
+                to_section(s, h, q).start()
+            if h > 0:
+                add_sections(s, h - 1)
+            if h == 0 and s + 1 < steps:
+                pass_on(s + 1, range(1))
+        add_sections(s, halves - 1)
         if s >= 1:
             finish(s - 1)
     finish(steps - 1)
     for s in range(max(0, steps - 2), steps):
-        for h in range(halves):
-            for k in range(1, blocks):
-                scatter(s, h, k).wait_send()
-    last = pltpu.make_async_copy(pair_ref.at[:, :, columns(me)], pair_all.at[me], keep_sem.at[2])
+        wait_sent(s)
+    last = pltpu.make_async_copy(pair_ref.at[:, :, columns(me)], pair_all.at[me], keep_sem.at[1])
     last.start()
     for s in range(steps):
         for way in range(2):
@@ -275,12 +305,11 @@
 
                 @pl.when(sends(way, j))
                 def _(s=s, way=way, j=j):
-                    gather(s, way, j).wait_send()
+                    for p in range(pieces):
+                        gather(s, way, j, p).wait_send()
 
     for k in range(1, blocks):
         send_lm(k).wait()
-    for k in range(1, n_t):
-        send_gram(k).wait()
     for s in range(steps - 1):
         for a in range(2):
             for k in range(1, blocks):
@@ -290,10 +319,10 @@
 
 
 def train_kernel(
-    n_t, n_dp, n_sec, scale, pair_ref, lm_ref, down_ref, up_all, up_ref, gram_all, lm_all, pair_all,
+    n_t, n_dp, n_sec, scale, pair_ref, lm_ref, down_ref, up_all, up_ref, lm_all, pair_all,
     grad_down_ref, grad_up_ref,
-    down, ups, gsum, gram_got, both, both_all, inner, inner_all, lms, pairs,
-    in_sem, gs_sem, gr_sem, bs_sem, br_sem, is_sem, ir_sem,
+    down, ups, both, both_all, inner, inner_all, lms, pairs,
+    in_sem, bs_sem, br_sem, is_sem, ir_sem,
 ):
     blocks = n_dp * n_sec
     count = pair_ref.shape[1]
@@ -325,72 +354,67 @@
         pl.semaphore_signal(barrier, inc=1, device_id=peer(k), device_id_type=MESH)
     pl.semaphore_wait(barrier, n_t - 1 + blocks - 1)
 
-    def send_gram(k):
+    def send_both(r, k):
         return pltpu.make_async_remote_copy(
-            src_ref=gsum, dst_ref=gram_got.at[section],
-            send_sem=gs_sem.at[k - 1], recv_sem=gr_sem.at[k - 1],
-            device_id={"section": lax.rem(section + k, n_sec)}, device_id_type=MESH,
-        )
-
-    def send_both(k):
+            src_ref=both.at[r], dst_ref=both_all.at[r, t],
+            send_sem=bs_sem.at[r, k - 1], recv_sem=br_sem.at[r, k - 1],
+            device_id={"tensor": lax.rem(t + k, n_t)}, device_id_type=MESH,
+        )
+
+    def summed(r, value):
+        both[r] = value
+        both_all[r, t] = value
+        for k in range(1, n_t):
+            send_both(r, k).start()
+        for k in range(1, n_t):
+            send_both(r, k).wait()
+        total = both_all[r, 0]
+        for i in range(1, n_t):
+            total += both_all[r, i]
+        return total
+
+    def send_inner(r, k):
         return pltpu.make_async_remote_copy(
-            src_ref=both, dst_ref=both_all.at[t],
-            send_sem=bs_sem.at[k - 1], recv_sem=br_sem.at[k - 1],
-            device_id={"tensor": lax.rem(t + k, n_t)}, device_id_type=MESH,
-        )
-
-    def send_inner(k):
-        return pltpu.make_async_remote_copy(
-            src_ref=inner, dst_ref=inner_all.at[me],
-            send_sem=is_sem.at[k - 1], recv_sem=ir_sem.at[k - 1],
+            src_ref=inner.at[r], dst_ref=inner_all.at[r, me],
+            send_sem=is_sem.at[r, k - 1], recv_sem=ir_sem.at[r, k - 1],
             device_id=peer(k), device_id_type=MESH,
         )
 
-    gsum[...] = sum(gram_all[i] for i in range(n_t))
-    gram_got[section] = gsum[...]
-    for k in range(1, n_sec):
-        send_gram(k).start()
-    loads[0].wait()
-    both[:, rank_width:] = lax.dot_general(
-        pair_ref[1], ups[...], (((1,), (1,)), ((), ())), preferred_element_type=F32
-    )
     loads[1].wait()
     pre = jnp.dot(pair_ref[0], down[2], preferred_element_type=F32)
     for c in range(2):
         pre += jnp.dot(lm_ref[c], down[c], preferred_element_type=F32)
-    both[:, :rank_width] = pre
-    both_all[t] = both[...]
-    for k in range(1, n_t):
-        send_both(k).start()
-    for k in range(1, n_sec):
-        send_gram(k).wait()
-    for k in range(1, n_t):
-        send_both(k).wait()
-    total = both_all[0]
-    for i in range(1, n_t):
-        total += both_all[i]
-    gram = gram_got[0]
-    for i in range(1, n_sec):
-        gram += gram_got[i]
-    pre, goal = total[:, :rank_width], total[:, rank_width:]
+    pre = summed(0, pre)
     sigma = jax.nn.sigmoid(pre)
     gated = (pre * sigma).astype(BF16)
-    back = jnp.dot(
-        gated.astype(F32), gram, precision=lax.Precision.HIGHEST, preferred_element_type=F32
-    ) - goal
-    back = back / scale
-    inner[:, :rank_width] = gated
-    inner[:, rank_width:] = (back * sigma * (1.0 + pre * (1.0 - sigma))).astype(BF16)
-    inner_all[me] = inner[...]
+    inner[0] = gated
+    inner_all[0, me] = gated
     for k in range(1, blocks):
-        send_inner(k).start()
+        send_inner(0, k).start()
+    loads[0].wait()
+    back = jnp.zeros((count, rank_width), F32)
+    cut = min(1024, width)
+    for c in range(0, ups.shape[1], cut):
+        part = ups[:, pl.ds(c, cut)]
+        pred = jnp.dot(gated, part, preferred_element_type=F32)
+        away = ((pred - pair_ref[1, :, pl.ds(c, cut)].astype(F32)) / scale).astype(BF16)
+        back += lax.dot_general(
+            away, part, (((1,), (1,)), ((), ())), preferred_element_type=F32
+        )
+    back = summed(1, back)
+    dpre = (back * sigma * (1.0 + pre * (1.0 - sigma))).astype(BF16)
+    inner[1] = dpre
+    inner_all[1, me] = dpre
+    for k in range(1, blocks):
+        send_inner(1, k).start()
     loads[2].wait()
     loads[3].wait()
     for k in range(1, blocks):
-        send_inner(k).wait()
+        send_inner(0, k).wait()
+        send_inner(1, k).wait()
     rows = blocks * count
-    gated = inner_all[:, :, :rank_width].reshape(rows, rank_width)
-    dpre = inner_all[:, :, rank_width:].reshape(rows, rank_width)
+    gated = inner_all[0].reshape(rows, rank_width)
+    dpre = inner_all[1].reshape(rows, rank_width)
     tile = min(512, width)
 
     def body(i, _):
@@ -413,9 +437,8 @@
 
 
 def fits(mesh_shape, attended, w_out, residual):
-    blocks = mesh_shape["dp"] * mesh_shape["section"]
     whole = attended.shape[1] % 16 == 0 and residual.shape[1] % 32 == 0
-    return whole and w_out.shape[1] % 1024 == 0 and mesh_shape["tensor"] > 1 and blocks > 1
+    return whole and w_out.shape[1] % 1024 == 0 and min(mesh_shape.values()) > 1
 
 
 def project_plain(attended, w_out, residual):
@@ -425,7 +448,7 @@
     return (residual.astype(F32) + summed).astype(BF16)
 
 
-def project(mesh_shape, attended, w_out, residual, choose, low_mid, gram):
+def project(mesh_shape, attended, w_out, residual, choose, low_mid):
     steps, rows, depth = attended.shape
     cols = w_out.shape[1]
     n_t, n_dp, n_sec = mesh_shape["tensor"], mesh_shape["dp"], mesh_shape["section"]
@@ -444,30 +467,31 @@
             jax.ShapeDtypeStruct((2, count, cols), BF16),
             spread,
             spread,
-            jax.ShapeDtypeStruct((n_t,) + gram.shape, F32),
         ),
-        in_specs=[hbm, hbm, vmem, vmem, hbm, hbm],
-        out_specs=(vmem, vmem, hbm, hbm, hbm),
+        in_specs=[hbm, hbm, vmem, vmem, hbm],
+        out_specs=(vmem, vmem, hbm, hbm),
         scratch_shapes=[
             pltpu.VMEM((steps, n_t, rows, depth), BF16),
             pltpu.VMEM((depth, cols), BF16),
             pltpu.VMEM((n_t * rows, 512), F32),
-            pltpu.VMEM((2, halves, blocks - 1, owned, half), BF16),
-            pltpu.VMEM((2, owned, cols), F32),
-            pltpu.VMEM((steps, halves, blocks - 1, owned, half), BF16),
+            pltpu.VMEM((2, halves, n_sec - 1, n_dp, owned, half), BF16),
+            pltpu.VMEM((2, n_dp, owned, cols), F32),
+            pltpu.VMEM((steps, halves, n_sec - 1, n_dp, owned, half), BF16),
+            pltpu.VMEM((2, halves, n_dp - 1, owned, half), BF16),
+            pltpu.VMEM((steps, halves, n_dp - 1, owned, half), BF16),
             dma((halves,)),
             dma((steps,)),
-            dma((steps, 2, n_t - 1)),
-            dma((steps, 2, n_t - 1)),
-            dma((steps, halves, blocks - 1)),
-            dma((steps, halves, blocks - 1)),
+            dma((steps, 2, n_t - 1, 2)),
+            dma((steps, 2, n_t - 1, 2)),
+            dma((steps, halves, n_sec - 1)),
+            dma((steps, halves, n_sec - 1)),
+            dma((steps, halves, n_dp - 1)),
+            dma((steps, halves, n_dp - 1)),
             dma((blocks - 1,)),
             dma((blocks - 1,)),
             dma((2, steps - 1, blocks - 1)),
             dma((2, steps - 1, blocks - 1)),
-            dma((n_t - 1,)),
-            dma((n_t - 1,)),
-            dma((3,)),
+            dma((2,)),
         ],
         compiler_params=pltpu.CompilerParams(
             collective_id=0, has_side_effects=True, vmem_limit_bytes=62 * 2**20
@@ -477,48 +501,43 @@
             bytes_accessed=2 * w_out.size,
             transcendentals=0,
         ),
-    )(attended, w_out, residual, choose, low_mid, gram)
-
-
-def train(mesh_shape, scale, pair, low_mid, down_full, up_full, up_map, gram_all, lm_all, pair_all):
+    )(attended, w_out, residual, choose, low_mid)
+
+
+def train(mesh_shape, scale, pair, low_mid, down_full, up_full, up_map, lm_all, pair_all):
     n_t, n_dp, n_sec = mesh_shape["tensor"], mesh_shape["dp"], mesh_shape["section"]
     blocks = n_dp * n_sec
     count = pair.shape[1]
     rank_width, width = up_map.shape
     dma = pltpu.SemaphoreType.DMA
     hbm, vmem = pl.BlockSpec(memory_space=pl.ANY), pl.BlockSpec(memory_space=pltpu.VMEM)
-    square = (rank_width, rank_width)
     return pl.pallas_call(
         functools.partial(train_kernel, n_t, n_dp, n_sec, scale),
         out_shape=(
             jax.ShapeDtypeStruct((3, width, rank_width), BF16),
             jax.ShapeDtypeStruct((rank_width, width), BF16),
         ),
-        in_specs=[vmem, vmem, hbm, hbm, vmem, vmem, hbm, hbm],
+        in_specs=[vmem, vmem, hbm, hbm, vmem, hbm, hbm],
         out_specs=(vmem, vmem),
         scratch_shapes=[
             pltpu.VMEM(down_full.shape, BF16),
             pltpu.VMEM(up_full.shape, BF16),
-            pltpu.VMEM(square, F32),
-            pltpu.VMEM((n_sec,) + square, F32),
-            pltpu.VMEM((count, 2 * rank_width), F32),
-            pltpu.VMEM((n_t, count, 2 * rank_width), F32),
-            pltpu.VMEM((count, 2 * rank_width), BF16),
-            pltpu.VMEM((blocks, count, 2 * rank_width), BF16),
+            pltpu.VMEM((2, count, rank_width), F32),
+            pltpu.VMEM((2, n_t, count, rank_width), F32),
+            pltpu.VMEM((2, count, rank_width), BF16),
+            pltpu.VMEM((2, blocks, count, rank_width), BF16),
             pltpu.VMEM(lm_all.shape, BF16),
             pltpu.VMEM(pair_all.shape, BF16),
             dma((4,)),
-            dma((max(1, n_sec - 1),)),
-            dma((max(1, n_sec - 1),)),
-            dma((n_t - 1,)),
-            dma((n_t - 1,)),
-            dma((blocks - 1,)),
-            dma((blocks - 1,)),
+            dma((2, n_t - 1)),
+            dma((2, n_t - 1)),
+            dma((2, blocks - 1)),
+            dma((2, blocks - 1)),
         ],
         compiler_params=pltpu.CompilerParams(
             collective_id=1, has_side_effects=True, vmem_limit_bytes=48 * 2**20
         ),
-    )(pair, low_mid, down_full, up_full, up_map, gram_all, lm_all, pair_all)
+    )(pair, low_mid, down_full, up_full, up_map, lm_all, pair_all)
 
 
 def on_device(
@@ -569,14 +588,14 @@
     down_full = lax.all_gather(down_map, "section", axis=1, tiled=True)
     up_full = lax.all_gather(up_map, "section", axis=1, tiled=True)
     gram = jnp.einsum("kj,lj->kl", up_map, up_map, preferred_element_type=F32)
+    queries, low_mid = lax.optimization_barrier((queries, low_mid))
     attended = attend(queries, cache, fresh_kv, lengths)
     if kernels:
-        top_hidden, pair, lm_all, pair_all, gram_all = project(
-            mesh_shape, attended, w_out, residual, choose, low_mid, gram
+        top_hidden, pair, lm_all, pair_all = project(
+            mesh_shape, attended, w_out, residual, choose, low_mid
         )
         grad_down, grad_up = train(
-            mesh_shape, steps - 1, pair, low_mid, down_full, up_full, up_map,
-            gram_all, lm_all, pair_all,
+            mesh_shape, steps - 1, pair, low_mid, down_full, up_full, up_map, lm_all, pair_all
         )
         return top_hidden, grad_down, grad_up
 

time: 321 us -> 269 us (0.84)
  Pallas kernels: 276 us -> 234 us
  local copies, waits for them, and re-layouts: 21.7 us -> 12.6 us
    pallas_call x1, Pallas kernels: 197 us -> 157 us  [project(): pl.pallas_call(functools.partial(project_kernel, n_t, n_dp, n_sec), out_s...]
    unnamed x27, local copies, waits for them, and re-layouts: 14.8 us -> 9.03 us
  transfers between devices with their start and end apart: 2 -> 2, of which waited for: 0 -> 0; matrix products, arithmetic and copies ran while one was open for 5% -> 4% of each run, Pallas kernels for 66% -> 64%
where the time goes in v3:
time: 269 us
  Pallas kernels  234 us (87%)
  between operations  14.2 us (5%)
  local copies, waits for them, and re-layouts  12.6 us (5%)
  matrix products  4.07 us (2%)
    pallas_call x1, Pallas kernels, project(): pl.pallas_call(functools.partial(project_kernel, n_t, n_dp, n_sec), out_s...  157 us
    pallas_call x1, Pallas kernels, train(): pl.pallas_call(functools.partial(train_kernel, n_t, n_dp, n_sec, scale),...  62 us
    pallas_call x1, Pallas kernels, attend(): pl.pallas_call(functools.partial(attend_kernel, group), grid=(kv, rows //...  15.2 us
    unnamed x27, local copies, waits for them, and re-layouts  9.03 us
  transfers between devices with their start and end apart: 2, of which 0 were waited for; matrix products, arithmetic and copies ran while one was open for 4% of the time, Pallas kernels for 64%

profile of v3, /device:TPU:9, one launch (start us, length us, event | category | flops | bytes accessed | tf_op | source)
XLA Modules:
  0.0 269.0 jit_solution(17374639739263586792)
XLA Ops:
  7.2 0.7 all-gather.5.cloned.1.call-update
  8.0 0.7 all-gather.3.cloned.1.call-update
  8.8 0.2 reduce_window_sum.11
  9.0 1.9 convolution_convert_fusion
  10.9 2.2 convolution_convert_fusion.1
  13.1 1.3 pad_maximum_fusion.lm_ref
  14.4 0.5 copy.16
  14.9 0.6 copy.13
  15.5 0.2 copy.20
  15.7 0.2 pad.4.fresh_ref
  15.9 0.1 compare_select_fusion.bias_ref
  16.1 0.4 copy-done.2
  16.4 15.2 %shard_map.121 = bf16[64,2,64,128]{3,2,1,0:T(8,128)(2,1)S(1)} custom-call(bf16[64,2,64,128]{3,2,1,0:T(8,128)(2,1)S(1)} %bitcast.25, bf16[2,2,64,256,128]{4,3,2,1,0:T(8,128)(2,1)S(1)} %copy-done.2, bf16[2,2,64,16,128]{4,3,2,1,0:T(8,128)(2,1)S(1)} %pad.4.fresh_ref, f32[64,1,256]{2,1,0:T(1,128)S(1)} %compare_select_fusion.bias_ref), custom_call_target="tpu_custom_call" | custom-call | flops 1073741824 | bytes 20971520 | tf_op jit(solution)/shard_map/pallas_call | solution.py:51
  31.6 0.4 copy.19
  32.0 2.3 reshape.65.att_ref
  34.3 0.6 fusion.5.choose_ref
  34.9 157.2 %shard_map.122 = (bf16[4,64,4096]{2,1,0:T(8,128)(2,1)}, bf16[2,96,4096]{2,1,0:T(8,128)(2,1)}, bf16[4,2,96,2048]{3,2,1,0:T(8,128)(2,1)}, bf16[4,2,96,2048]{3,2,1,0:T(8,128)(2,1)}) custom-call(bf16[4,64,4096]{2,1,0:T(8,128)(2,1)} %reshape.65.att_ref, bf16[4096,4096]{1,0:T(8,128)(2,1)} %w_ref.1, bf16[4,64,4096]{2,1,0:T(8,128)(2,1)} %res_ref.1, ...), custom_call_target="tpu_custom_call" | custom-call | flops 34359738368 | bytes 33554432 | tf_op jit(solution)/shard_map/pallas_call | solution.py:463
  192.3 1.2 copy-done.4
  193.5 1.4 copy-done.5
  194.9 62.0 %shard_map.123 = (bf16[3,2048,256]{2,1,0:T(8,128)(2,1)}, bf16[256,2048]{1,0:T(8,128)(2,1)S(1)}) custom-call(bf16[2,96,4096]{2,1,0:T(8,128)(2,1)S(1)} %copy-done.5, bf16[2,96,4096]{2,1,0:T(8,128)(2,1)S(1)} %copy-done.3, bf16[3,4096,256]{2,1,0:T(8,128)(2,1)} %all-gather.3.cloned.1.call-done.down_ref, bf16[256,4096]{1,0:T(8,128)(2,1)} %all-gather.5.cloned.1.call-done.up_all, ...), custom_call_target="tpu_custom_call" | custom-call | tf_op jit(solution)/shard_map/pallas_call | solution.py:514
  256.9 1.3 copy.24
  258.2 1.3 copy-done.6
  259.5 1.7 copy.25
  261.2 1.0 copy.26
  (25 shorter events, 0.3 us)
Async XLA Ops:
  7.2 1.5 copy-start
  7.2 185.0 %all-gather.5.cloned.1.call-start = ((), (), s32[]{:S(2)}) async-start(), calls=%async_computation.1 | async-start | bytes 3145728 | tf_op jit(solution)/shard_map/all_gather | solution.py:589
  7.9 184.3 %all-gather.3.cloned.1.call-start = ((), (), s32[]{:S(2)}) async-start(), calls=%async_computation | async-start | bytes 9437184 | tf_op jit(solution)/shard_map/all_gather | solution.py:588
  8.0 6.4 %copy-start.7 = (bf16[4,64,4096]{2,1,0:T(8,128)(2,1)S(1)}, bf16[4,64,4096]{2,1,0:T(8,128)(2,1)}, u32[]{:S(2)}) copy-start(bf16[4,64,4096]{2,1,0:T(8,128)(2,1)} %param.10) | copy-start | bytes 6291460
  8.0 7.5 %copy-start.9 = (bf16[4,2,2,64,128]{4,3,2,1,0:T(8,128)(2,1)S(1)}, bf16[4,2,2,64,128]{4,3,2,1,0:T(8,128)(2,1)}, u32[]{:S(2)}) copy-start(bf16[4,2,2,64,128]{4,3,2,1,0:T(8,128)(2,1)} %param.12) | copy-start | bytes 786436
  9.0 7.4 %copy-start.2 = (bf16[2,2,64,256,128]{4,3,2,1,0:T(8,128)(2,1)S(1)}, bf16[2,2,64,256,128]{4,3,2,1,0:T(8,128)(2,1)}, u32[]{:S(2)}) copy-start(bf16[2,2,64,256,128]{4,3,2,1,0:T(8,128)(2,1)} %cache_ref.1) | copy-start | bytes 50331652
  14.9 1.1 copy-start.10
  34.9 157.3 %copy-start.3 = (bf16[2,96,4096]{2,1,0:T(8,128)(2,1)S(1)}, bf16[2,96,4096]{2,1,0:T(8,128)(2,1)}, u32[]{:S(2)}) copy-start(bf16[2,96,4096]{2,1,0:T(8,128)(2,1)} %pad_maximum_fusion.lm_ref) | copy-start | bytes 4718596
  192.2 1.2 copy-start.4
  193.5 1.4 copy-start.5
  194.9 62.0 %copy-start.8 = (bf16[4,64,4096]{2,1,0:T(8,128)(2,1)S(1)}, bf16[4,64,4096]{2,1,0:T(8,128)(2,1)}, u32[]{:S(2)}) copy-start(bf16[4,64,4096]{2,1,0:T(8,128)(2,1)} %get-tuple-element.22) | copy-start | bytes 6291460
  256.9 2.6 copy-start.6
  259.5 2.6 copy-start.1
Sparse Core Ops, SparseCore 0:
  9.6 12.4 all-gather.4
  23.6 18.9 all-gather.2
